TPU v7x, 128 devices: a whole 4x4x4 slice. The times are simulated.
128 devices in a mesh: img: 8 (over z, y_hi), ref: 16 (over x, y_lo, core).
Axes of the slice: x: 4, y: 4 (y_hi: 2, y_lo: 2; y = y_hi * 2 + y_lo), z: 4, core: 2. Of those that a mesh axis runs over, the one named last changes fastest.
Arguments:
- images: bfloat16 [8192, 9216], P(('img', 'ref')), may hold values from -96 to 96
- references: bfloat16 [6912, 9216], P('ref'), may hold values from -0.5 to 0.5
- class_prior: float32 [192], P('ref'), may hold values from 0.2 to 5
Outputs:
- class_sums: float32 [192, 9216], P('ref', 'img')
- class_weights: float32 [192], P('ref')
All inputs are finite; a program needn't handle non-finite values.
Results may differ from a plain program's by a relative error of at most 0.0021.
Values may be sent and summed in bfloat16 or wider, within the bound.
A program may use at most 128 MiB of HBM per device.

v0:
```python
import jax
import jax.numpy as jnp
from jax import lax
from jax.sharding import PartitionSpec as P

ANG = 144


def unturn(stacked, shift_size):
    classes_here, rotations, columns = stacked.shape
    cycles = stacked.reshape(classes_here, rotations, columns // ANG, ANG)
    doubled = jnp.concatenate([cycles, cycles], axis=3)
    result = doubled[:, 0, :, 0:ANG]
    for turn_index in range(1, rotations):
        start_col = turn_index * shift_size
        result = result + doubled[:, turn_index, :, start_col : start_col + ANG]
    return result.reshape(classes_here, columns)


def per_device(images, references, class_prior):
    local_refs, pixels = references.shape
    classes_here = class_prior.shape[0]
    rotations = local_refs // classes_here
    shift_size = ANG // rotations
    half_norm = 0.5 * jnp.einsum(
        "jp,jp->j", references, references, preferred_element_type=jnp.float32
    )
    offsets = (jnp.log(class_prior)[:, None] - half_norm.reshape(classes_here, rotations)).reshape(
        local_refs
    )
    gathered = lax.all_gather(images, "ref", axis=0, tiled=True)
    products = lax.dot_general(
        gathered, references, (((1,), (1,)), ((), ())), preferred_element_type=jnp.float32
    )
    scores = products + offsets
    local_max = jnp.max(scores, axis=1)
    top_score = lax.pmax(local_max, "ref")
    denominator = lax.psum(jnp.sum(jnp.exp(scores - top_score[:, None]), axis=1), "ref")
    weights = (jnp.exp(scores - top_score[:, None]) / denominator[:, None]).astype(jnp.bfloat16)
    local_mass = (
        jnp.sum(weights.astype(jnp.float32), axis=0).reshape(classes_here, rotations).sum(axis=1)
    )
    class_weights = lax.psum(local_mass, "img")
    sums = lax.dot_general(
        weights, gathered, (((0,), (0,)), ((), ())), preferred_element_type=jnp.float32
    )
    reduced = lax.psum_scatter(sums, "img", scatter_dimension=1, tiled=True)
    class_sums = unturn(reduced.reshape(classes_here, rotations, -1), shift_size)
    return (class_sums, class_weights)


def solution(mesh):
    placed = (P(("img", "ref"), None), P("ref", None), P("ref"))
    return jax.shard_map(
        per_device,
        mesh=mesh,
        in_specs=placed,
        out_specs=(P("ref", "img"), P("ref")),
        check_vma=False,
    )
```

profile of v0, /device:TPU:0, one launch (start us, length us, event | category | flops | bytes accessed | tf_op | source)
XLA Modules:
  0.0 434.1 jit_solution(321626960868306678)
XLA Ops:
  8.8 4.9 %fusion = f32[432]{0:T(512)S(1)} fusion(bf16[432,9216]{1,0:T(8,128)(2,1)} %param.4), kind=kLoop, calls=%fused_computation.1 | loop fusion | flops 11943504 | bytes 7964352 | tf_op jit(solution)/shard_map/jp,jp->j/dot_general | solution.py:25
  13.7 100.0 %all-gather.2.cloned.1.call-done = bf16[1024,9216]{1,0:T(8,128)(2,1)} async-done(((bf16[64,9216]{1,0:T(8,128)(2,1)}), bf16[1024,9216]{1,0:T(8,128)(2,1)}) %all-gather.2.cloned.1.call-update) | async-done | bytes 18874384 | tf_op jit(solution)/shard_map/all_gather | solution.py:31
  113.7 14.2 %add_reduce_fusion = (f32[1024]{0:T(1024)S(1)}, f32[1024,432]{0,1:T(8,128)S(1)}) fusion(f32[432]{0:T(512)S(1)} %multiply_subtract_fusion, bf16[1024,9216]{1,0:T(8,128)(2,1)} %all-gather.2.cloned.1.call-done, bf16[432,9216]{1,0:T(8,128)(2,1)} %param.4), kind=kOutput, calls=%fused_computation.5 | convolution fusion | flops 8154610688 | bytes 28612288 | tf_op jit(solution)/shard_map/dot_general | solution.py:32
  127.9 29.8 %pmax.7 = f32[1024]{0:T(1024)S(1)} all-reduce(f32[1024]{0:T(1024)S(1)} %get-tuple-element.22), channel_id=1, replica_groups=mesh['img'=8,'ref'=16] {'ref'}, use_global_device_ids=true, to_apply=%region_1.0 | all-reduce | flops 1024 | bytes 8192 | tf_op jit(solution)/shard_map/pmax | solution.py:37
  158.0 27.1 %psum.14 = f32[1024]{0:T(1024)S(1)} all-reduce(f32[1024]{0:T(1024)S(1)} %fusion.1), channel_id=1, replica_groups=mesh['img'=8,'ref'=16] {'ref'}, use_global_device_ids=true, to_apply=%region_3.0 | all-reduce | flops 1024 | bytes 8192 | tf_op jit(solution)/shard_map/psum | solution.py:38
  185.7 17.5 %fusion.2 = f32[432,9216]{1,0:T(8,128)} fusion(bf16[1024,432]{0,1:T(8,128)(2,1)S(1)} %get-tuple-element.3, bf16[1024,9216]{1,0:T(8,128)(2,1)} %all-gather.2.cloned.1.call-done), kind=kOutput, calls=%fused_computation.44 | convolution fusion | flops 8153726976 | bytes 35684352 | tf_op jit(solution)/shard_map/dot_general | solution.py:44
  203.5 25.3 %psum.15 = f32[12]{0:T(128)} all-reduce(f32[12]{0:T(128)S(1)} %reduce_sum.29), channel_id=1, replica_groups=mesh['img'=8,'ref'=16] {'img'}, use_global_device_ids=true, to_apply=%region_7.0 | all-reduce | flops 12 | bytes 96 | tf_op jit(solution)/shard_map/psum | solution.py:43
  228.8 169.3 %reduce-scatter.2.cloned.1.call-done = f32[432,1152]{1,0:T(8,128)} async-done(((f32[432,9216]{1,0:T(8,128)}), f32[432,1152]{1,0:T(8,128)}) %reduce-scatter.2.cloned.1.call-update) | async-done | bytes 1990672 | tf_op jit(solution)/shard_map/reduce_scatter | solution.py:47
  398.0 3.5 reshape_reshape.3
  401.6 1.5 maximum_add_fusion
  403.8 1.4 pad_maximum_fusion.18
  405.2 1.4 pad_maximum_fusion.17
  406.6 1.0 reshape.71
  407.6 1.0 squeeze.128
  408.6 1.0 squeeze.111
  409.6 1.0 squeeze.110
  410.6 1.0 squeeze.126
  411.6 1.0 squeeze.118
  412.6 1.0 squeeze.122
  413.6 1.0 squeeze.117
  414.6 1.0 squeeze.124
  415.6 1.0 squeeze.116
  416.6 1.0 squeeze.121
  417.6 1.0 squeeze.115
  418.6 1.0 squeeze.125
  419.6 1.0 squeeze.114
  420.5 1.0 squeeze.120
  421.5 1.0 squeeze.113
  422.5 1.0 squeeze.123
  423.5 1.0 squeeze.112
  424.5 1.0 squeeze.119
  425.5 1.0 squeeze.127
  (14 shorter events, 4.2 us)
Async XLA Ops:
  7.2 106.5 %all-gather.2.cloned.1.call-start = ((), (), s32[]{:S(2)}) async-start(), calls=%async_computation.1 | async-start | bytes 20054016 | tf_op jit(solution)/shard_map/all_gather | solution.py:31
  7.9 390.1 %reduce-scatter.2.cloned.1.call-start = ((), (), s32[]{:S(2)}) async-start(), calls=%async_computation.2 | async-start | bytes 17915904 | tf_op jit(solution)/shard_map/reduce_scatter | solution.py:47
Sparse Core Ops, SparseCore 0:
  9.7 103.9 all-gather.1
  203.4 194.5 reduce-scatter.1
where the time goes:
time: 435 us; the launch traced here: 434 us
  waiting for transfers between devices  270 us (62%)
  blocking collectives  82.2 us (19%)
  matrix products  31.7 us (7%)
  local copies, waits for them, and re-layouts  24.3 us (6%)
  between operations  14.1 us (3%)
  other arithmetic  11.7 us (3%)
    reduce_scatter x1, waiting for transfers between devices, per_device(): reduced = lax.psum_scatter(sums, 'img', scatter_dimension=1, tiled=True)  169 us
    all_gather x1, waiting for transfers between devices, per_device(): gathered = lax.all_gather(images, 'ref', axis=0, tiled=True)  100 us
    pmax x1, blocking collectives, per_device(): top_score = lax.pmax(local_max, 'ref')  29.8 us
    psum x1, blocking collectives, per_device(): lax.psum(jnp.sum(jnp.exp(scores - top_score[:, None]), axis=1), 'ref')  27.1 us
    psum x1, blocking collectives, per_device(): class_weights = lax.psum(local_mass, 'img')  25.3 us
    squeeze x19, local copies, waits for them, and re-layouts, unturn(): result = result + doubled[:, turn_index, :, start_col:start_col + ANG]  18.9 us
    dot_general x1, matrix products, per_device(): lax.dot_general(weights, gathered, (((0,), (0,)), ((), ())), preferred_el...  17.5 us
    dot_general x1, matrix products, per_device(): lax.dot_general(gathered, references, (((1,), (1,)), ((), ())), preferred...  14.2 us
  transfers between devices with their start and end apart: 2, of which 2 were waited for; matrix products, arithmetic and copies ran while one was open for 1% of the time, Pallas kernels for 0%

commit v1 on v0

v1 whole, which is shorter than its diff:
```python
import math
import numpy as np
import jax
import jax.numpy as jnp
from jax import lax
from jax.sharding import PartitionSpec as P

ANG = 144
ROT = 36
TURN = 4


def real_dft():
    b = np.arange(ROT)
    rows = []
    for f in range(1, ROT // 2):
        rows.append(np.cos(2 * np.pi * f * b / ROT))
        rows.append(-np.sin(2 * np.pi * f * b / ROT))
    rows = [np.ones(ROT), (-1.0) ** b] + rows
    return (np.array(rows)).astype(np.float32)


def real_idft():
    b = np.arange(ROT)
    rows = [np.ones(ROT) / ROT, (-1.0) ** b / ROT]
    for f in range(1, ROT // 2):
        rows.append(2 * np.cos(2 * np.pi * f * b / ROT) / ROT)
        rows.append(-2 * np.sin(2 * np.pi * f * b / ROT) / ROT)
    return np.array(rows).T.astype(np.float32)


def per_device(images, references, class_prior):
    hi = lax.Precision.HIGHEST
    classes_here = class_prior.shape[0]
    n_img, pixels = images.shape
    rad = pixels // ANG
    templates = references.reshape(classes_here, ROT, pixels)[:, 0]
    half_norm = 0.5 * jnp.sum(jnp.square(templates.astype(jnp.float32)), axis=1)
    offset = jnp.log(class_prior) - half_norm
    offsets = lax.all_gather(offset, "ref", axis=0, tiled=True)
    tall = lax.all_gather(templates, "ref", axis=0, tiled=True)
    k = tall.shape[0]
    dft, idft = real_dft(), real_idft()
    x5 = images.reshape(n_img, rad, ROT, TURN).transpose(2, 0, 1, 3).reshape(ROT, n_img, rad * TURN)
    t5 = tall.reshape(k, rad, ROT, TURN).transpose(2, 0, 1, 3).reshape(ROT, k, rad * TURN)
    xh = jnp.einsum("jb,bnc->jnc", dft, x5.astype(jnp.float32), precision=hi)
    th = jnp.einsum("jb,bkc->jkc", dft, t5.astype(jnp.float32), precision=hi)
    xr, xi = xh[0::2], xh[1::2]
    tr, ti = th[0::2], th[1::2]
    dot = lambda a, b: jnp.einsum("fkc,fnc->fkn", a, b, precision=hi)
    rr, ii = dot(tr, xr), dot(ti, xi)
    ri, ir = dot(tr[1:], xi[1:]), dot(ti[1:], xr[1:])
    sr = jnp.concatenate([rr[:1], rr[1:] + ii[1:]])
    si = jnp.concatenate([ii[:1], ri - ir])
    sh = jnp.stack([sr, si], axis=1).reshape(ROT, k, n_img)
    scores = jnp.einsum("rj,jkn->rkn", idft, sh, precision=hi) + offsets[None, :, None]
    top = jnp.max(scores, axis=(0, 1))
    e = jnp.exp(scores - top)
    weights = (e / jnp.sum(e, axis=(0, 1))).astype(jnp.bfloat16).astype(jnp.float32)
    mass = jnp.sum(weights, axis=(0, 2))
    class_weights = lax.psum_scatter(lax.psum(mass, "img"), "ref", scatter_dimension=0, tiled=True)
    wh = jnp.einsum("jr,rkn->jkn", dft, weights, precision=hi)
    wr, wi = wh[0::2], wh[1::2]
    dot2 = lambda a, b: jnp.einsum("fkn,fnc->fkc", a, b, precision=hi)
    cr = jnp.concatenate([dot2(wr[:1], xr[:1]), dot2(wr[1:], xr[1:]) + dot2(wi[1:], xi[1:])])
    ci = jnp.concatenate([dot2(wi[:1], xi[:1]), dot2(wr[1:], xi[1:]) - dot2(wi[1:], xr[1:])])
    c = jnp.stack([cr, ci], axis=1).reshape(ROT, k, rad, TURN)
    sums = jnp.einsum("bj,jkqc->kqbc", idft, c, precision=hi).reshape(k, pixels)
    sums = lax.psum_scatter(sums, "ref", scatter_dimension=0, tiled=True)
    class_sums = lax.psum_scatter(sums, "img", scatter_dimension=1, tiled=True)
    return (class_sums, class_weights)


def solution(mesh):
    placed = (P(("img", "ref"), None), P("ref", None), P("ref"))
    return jax.shard_map(
        per_device,
        mesh=mesh,
        in_specs=placed,
        out_specs=(P("ref", "img"), P("ref")),
        check_vma=False,
    )
```

time: 435 us -> 649 us (1.49); the launches traced: 434 us -> 637 us
  local copies, waits for them, and re-layouts: 24.3 us -> 208 us
  matrix products: 31.7 us -> 69 us
  waiting for transfers between devices: 270 us -> 249 us
    unnamed x2 -> x4, waiting for transfers between devices: 0.7 us -> 213 us
    reduce_scatter x1, waiting for transfers between devices: 169 us -> 36.2 us  [per_device(): class_sums = lax.psum_scatter(sums, 'img', scatter_dimension=1, tiled=True)]
    all_gather x1, waiting for transfers between devices: 100 us -> 0.01 us  [per_device(): tall = lax.all_gather(templates, 'ref', axis=0, tiled=True)]
    slice x0 -> x21, local copies, waits for them, and re-layouts: none -> 82.4 us  [the longest x2 44.2 us: per_device(): tr, ti = (th[0::2], th[1::2])]
    reshape x1 -> x8, local copies, waits for them, and re-layouts: 0.08 us -> 75.2 us  [the longest x2 26.8 us: per_device(): c = jnp.stack([cr, ci], axis=1).reshape(ROT, k, rad, TURN)]
    unnamed x0 -> x2, blocking collectives: none -> 60.5 us
    dot_general x2 -> x15, matrix products: 31.7 us -> 69 us  [the longest x4 22.4 us: per_device(): dot = lambda a, b: jnp.einsum('fkc,fnc->fkn', a, b, precision=hi)]
    pmax x1 -> x0, blocking collectives: 29.8 us -> none  [per_device(): top_score = lax.pmax(local_max, 'ref')]
  transfers between devices with their start and end apart: 2 -> 3, of which waited for: 2 -> 2; matrix products, arithmetic and copies ran while one was open for 1% -> 4% of each run, Pallas kernels for 0% -> 0%
where the time goes in v1:
time: 649 us; the launch traced here: 637 us
  waiting for transfers between devices  249 us (38%)
  local copies, waits for them, and re-layouts  208 us (32%)
  blocking collectives  85.7 us (13%)
  matrix products  69 us (11%)
  between operations  15.9 us (2%)
  other arithmetic  9.31 us (1%)
    unnamed x4, waiting for transfers between devices  213 us
    unnamed x2, blocking collectives  60.5 us
    slice x2, local copies, waits for them, and re-layouts, per_device(): tr, ti = (th[0::2], th[1::2])  44.2 us
    reduce_scatter x1, waiting for transfers between devices, per_device(): class_sums = lax.psum_scatter(sums, 'img', scatter_dimension=1, tiled=True)  36.2 us
    reshape x2, local copies, waits for them, and re-layouts, per_device(): c = jnp.stack([cr, ci], axis=1).reshape(ROT, k, rad, TURN)  26.8 us
    psum x1, blocking collectives, per_device(): lax.psum(mass, 'img')  25.2 us
    reshape x3, local copies, waits for them, and re-layouts, per_device(): tall.reshape(k, rad, ROT, TURN).transpose(2, 0, 1, 3)  24.3 us
    dot_general x4, matrix products, per_device(): dot = lambda a, b: jnp.einsum('fkc,fnc->fkn', a, b, precision=hi)  22.4 us
  transfers between devices with their start and end apart: 3, of which 2 were waited for; matrix products, arithmetic and copies ran while one was open for 4% of the time, Pallas kernels for 0%

profile of v1, /device:TPU:0, one launch (start us, length us, event | category | flops | bytes accessed | tf_op | source)
XLA Modules:
  0.0 636.5 jit_solution(5112398509001411555)
XLA Ops:
  7.2 8.7 %reshape.45 = bf16[12,36,9216]{2,1,0:T(8,128)(2,1)} reshape(bf16[432,9216]{1,0:T(8,128)(2,1)} %param.9) | data formatting | bytes 15925248 | tf_op jit(solution)/shard_map/reshape | solution.py:37
  23.8 3.4 copy.60
  29.8 4.8 slice.75
  34.6 4.9 slice.71
  46.0 30.8 %all-reduce = f32[192]{0:T(256)S(1)} all-reduce(f32[192]{0:T(256)S(1)} %subtract_dynamic-update-slice_fusion), channel_id=1, replica_groups=mesh['img'=8,'ref'=16] {'ref'}, use_global_device_ids=true, to_apply=%add | all-reduce | flops 192 | bytes 1536
  76.8 16.0 %copy.55 = bf16[192,1,9216]{0,2,1:T(8,128)(2,1)} copy(bf16[192,1,9216]{2,1,0:T(2,128)(2,1)} %all-gather.3.cloned.1.call-done) | data formatting | bytes 7077888 | tf_op jit(solution)/shard_map/all_gather | solution.py:41
  92.8 7.9 %reshape.46 = bf16[192,64,36,4]{0,3,2,1:T(4,128)(2,1)} reshape(bf16[192,1,9216]{0,2,1:T(8,128)(2,1)} %copy.55) | data formatting | bytes 7077888 | tf_op jit(solution)/shard_map/reshape | solution.py:45
  100.7 7.0 %copy.56 = bf16[36,192,64,4]{1,3,2,0:T(4,128)(2,1)} copy(bf16[36,192,64,4]{1,3,0,2:T(4,128)(2,1)} %bitcast.63) | data formatting | bytes 7077888 | tf_op jit(solution)/shard_map/transpose | solution.py:45
  107.7 8.5 %reshape.47 = bf16[36,192,256]{1,2,0:T(8,128)(2,1)} reshape(bf16[36,192,64,4]{1,3,2,0:T(4,128)(2,1)} %copy.56) | data formatting | bytes 7077888 | tf_op jit(solution)/shard_map/reshape | solution.py:45
  116.2 7.9 %copy.57 = bf16[36,192,256]{2,0,1:T(8,128)(2,1)} copy(bf16[36,192,256]{1,2,0:T(8,128)(2,1)} %reshape.47) | data formatting | bytes 7077888 | tf_op jit(solution)/shard_map/reshape | solution.py:45
  124.1 8.4 %fusion.39 = f32[36,192,256]{2,0,1:T(8,128)} fusion(f32[36,36,1]{1,0,2:T(8,128)S(1)} %copy-done.6, bf16[36,192,256]{2,0,1:T(8,128)(2,1)} %copy.57), kind=kOutput, calls=%fused_computation.56 | convolution fusion | flops 764411904 | bytes 10622016 | tf_op jit(solution)/shard_map/jb,bkc->jkc/dot_general | solution.py:47
  132.5 22.0 %slice.74 = f32[18,192,256]{2,0,1:T(8,128)} slice(f32[36,192,256]{2,0,1:T(8,128)} %fusion.39), slice={[1:36:2], [0:192:1], [0:256:1]} | slice | bytes 7077888 | tf_op jit(solution)/shard_map/slice | solution.py:49
  154.5 22.2 %slice.70 = f32[18,192,256]{2,0,1:T(8,128)} slice(f32[36,192,256]{2,0,1:T(8,128)} %fusion.39), slice={[0:36:2], [0:192:1], [0:256:1]} | slice | bytes 7077888 | tf_op jit(solution)/shard_map/slice | solution.py:49
  176.7 7.8 %fusion = f32[18,192,64]{1,2,0:T(8,128)S(1)} fusion(f32[18,192,256]{2,0,1:T(8,128)} %slice.74, f32[18,64,256]{2,0,1:T(8,128)} %slice.75), kind=kOutput, calls=%fused_computation.4 | convolution fusion | flops 679477248 | bytes 5603328 | tf_op jit(solution)/shard_map/fkc,fnc->fkn/dot_general | solution.py:50
  187.9 4.9 fusion.2
  194.0 5.1 fusion.4
  199.1 4.6 fusion.11
  204.9 4.3 add_reduce_fusion
  214.4 8.1 %slice.82 = f32[18,192,64]{1,0,2:T(8,128)} slice(f32[36,192,64]{1,0,2:T(8,128)} %fusion.14), slice={[0:36:2], [0:192:1], [0:64:1]} | slice | bytes 1769472 | tf_op jit(solution)/shard_map/slice | solution.py:63
  222.5 8.1 %slice.86 = f32[18,192,64]{1,0,2:T(8,128)} slice(f32[36,192,64]{1,0,2:T(8,128)} %fusion.14), slice={[1:36:2], [0:192:1], [0:64:1]} | slice | bytes 1769472 | tf_op jit(solution)/shard_map/slice | solution.py:63
  240.3 3.4 convolution_subtract_fusion
  243.8 3.7 convolution_add_fusion
  252.2 14.4 %copy.84 = f32[18,2,192,256]{2,1,0,3:T(2,128)} copy(f32[18,2,192,256]{3,2,0,1:T(8,128)} %pad_maximum_fusion) | data formatting | bytes 14155776 | tf_op jit(solution)/shard_map/reshape | solution.py:67
  266.6 12.4 %reshape.69 = f32[36,192,64,4]{1,0,3,2:T(8,128)} reshape(f32[18,2,192,256]{2,1,0,3:T(2,128)} %copy.84) | data formatting | bytes 14155776 | tf_op jit(solution)/shard_map/reshape | solution.py:67
  279.0 14.2 %convolution_bitcast_fusion = f32[192,64,36,4]{0,2,3,1:T(8,128)} fusion(f32[36,192,64,4]{1,0,3,2:T(8,128)} %reshape.69, f32[36,36,1,1]{1,0,3,2:T(8,128)S(1)} %copy-done.7), kind=kOutput, calls=%fused_computation.1 | convolution fusion | flops 764411904 | bytes 14160960 | tf_op jit(solution)/shard_map/bj,jkqc->kqbc/dot_general | solution.py:68
  293.2 11.9 %copy.81 = f32[192,64,36,4]{0,3,2,1:T(4,128)} copy(f32[192,64,36,4]{0,2,3,1:T(8,128)} %convolution_bitcast_fusion) | data formatting | bytes 14155776 | tf_op jit(solution)/shard_map/bj,jkqc->kqbc/transpose | solution.py:68
  305.1 12.0 %reshape.56 = f32[192,9216]{0,1:T(8,128)} reshape(f32[192,64,36,4]{0,3,2,1:T(4,128)} %copy.81) | data formatting | bytes 14155776 | tf_op jit(solution)/shard_map/reshape | solution.py:68
  317.8 212.6 %all-reduce.5.cloned.1.call-done = f32[192,9216]{0,1:T(8,128)} async-done(((f32[192,9216]{0,1:T(8,128)}), f32[192,9216]{0,1:T(8,128)}) %all-reduce.5.cloned.1.call-update) | async-done | bytes 7077904
  530.5 6.0 constant_dynamic-slice_fusion
  536.4 29.7 %all-reduce.2 = f32[192]{0:T(256)S(1)} all-reduce(f32[192]{0:T(256)S(1)} %get-tuple-element.6), channel_id=5, replica_groups=mesh['img'=8,'ref'=16] {'ref'}, use_global_device_ids=true, to_apply=%region_7.0.clone | all-reduce | flops 192 | bytes 1536
  566.2 25.2 %psum.8 = f32[12]{0:T(128)} all-reduce(f32[12]{0:T(128)S(1)} %dynamic-slice.4), channel_id=1, replica_groups=mesh['img'=8,'ref'=16] {'img'}, use_global_device_ids=true, to_apply=%region_6.0 | all-reduce | flops 12 | bytes 96 | tf_op jit(solution)/shard_map/psum | solution.py:61
  591.4 36.2 %reduce-scatter.3.cloned.1.call-done = f32[12,1152]{0,1:T(8,128)} async-done(((f32[12,9216]{0,1:T(8,128)}), f32[12,1152]{0,1:T(8,128)}) %reduce-scatter.3.cloned.1.call-update) | async-done | bytes 55312 | tf_op jit(solution)/shard_map/reduce_scatter | solution.py:70
  (72 shorter events, 43.6 us)
Async XLA Ops:
  7.2 11.3 %copy-start.5 = (bf16[64,9216]{1,0:T(8,128)(2,1)S(1)}, bf16[64,9216]{1,0:T(8,128)(2,1)}, u32[]{:S(2)}) copy-start(bf16[64,9216]{1,0:T(8,128)(2,1)} %param.8) | copy-start | bytes 3538948
  7.2 69.6 %all-gather.3.cloned.1.call-start = ((), (), s32[]{:S(2)}) async-start(), calls=%async_computation.2 | async-start | bytes 7520256 | tf_op jit(solution)/shard_map/all_gather | solution.py:41
  18.4 512.0 %all-reduce.5.cloned.1.call-start = ((), (), s32[]{:S(2)}) async-start(), calls=%async_computation.3 | async-start | bytes 18874368
  23.8 3.4 copy-start.6
  39.5 2.9 copy-start
  41.2 1.3 copy-start.9
  41.2 4.7 copy-start.10
  176.7 11.2 %slice-start = ((s8[4718592]{0:T(1024)(128)(4,1)}), s8[4194304]{0:T(1024)(128)(4,1)S(1)}, s32[]{:S(2)}) async-start(s8[4718592]{0:T(1024)(128)(4,1)} %bitcast.61), calls=%async_computation.4 | async-start | bytes 8388608
  184.5 9.5 %copy-start.3 = (f32[18,192,64]{1,2,0:T(8,128)}, f32[18,192,64]{1,2,0:T(8,128)S(1)}, u32[]{:S(2)}) copy-start(f32[18,192,64]{1,2,0:T(8,128)S(1)} %fusion) | copy-start | bytes 2654212
  184.5 3.4 slice-start.1
  184.5 3.4 copy-start.1
  192.8 1.0 copy-start.4
  199.1 4.6 slice-start.2
  199.1 4.6 slice-start.3
  204.2 0.7 copy-start.8
  230.6 2.8 copy-start.2
  266.6 12.4 %copy-start.7 = (f32[36,36,1,1]{1,0,3,2:T(8,128)S(1)}, f32[36,36,1,1]{1,0,3,2:T(8,128)}, u32[]{:S(2)}) copy-start(f32[36,36,1,1]{1,0,3,2:T(8,128)} %constant.30) | copy-start | bytes 15556
  317.1 310.5 %reduce-scatter.3.cloned.1.call-start = ((), (), s32[]{:S(2)}) async-start(), calls=%async_computation.1 | async-start | bytes 5308416 | tf_op jit(solution)/shard_map/reduce_scatter | solution.py:70
Sparse Core Ops, SparseCore 0:
  18.5 48.8 all-gather.2
  317.2 213.1 all-reduce.4
  536.6 91.0 reduce-scatter.2

commit v2 on v0

v2 whole, which is shorter than its diff:
```python
import math
import numpy as np
import jax
import jax.numpy as jnp
from jax import lax
from jax.experimental import pallas as pl
from jax.experimental.pallas import tpu as pltpu
from jax.sharding import PartitionSpec as P

ANG = 144
ROT = 36
TURN = 4
BAND = 1152
HALF = ROT // 2
F32 = jnp.float32
BF16 = jnp.bfloat16
MESH = pl.DeviceIdType.MESH

COS9 = [math.cos(2 * math.pi * m / 9) for m in range(9)]
SIN9 = [math.sin(2 * math.pi * m / 9) for m in range(9)]
ROOT3H = math.sqrt(3.0) / 2


def cos_sums(y0, e):
    t = e[0] + e[1] + e[3]
    top = y0 + e[2]
    base = y0 - 0.5 * e[2]
    out = [top + t]
    for f in (1, 2, 4):
        out.append(base + COS9[f % 9] * e[0] + COS9[2 * f % 9] * e[1] + COS9[4 * f % 9] * e[3])
    out.insert(3, top - 0.5 * t)
    return out


def sin_sums(o):
    h = ROOT3H * o[2]
    one = SIN9[1] * o[0] + SIN9[2] * o[1] + h + SIN9[4] * o[3]
    two = SIN9[2] * o[0] + SIN9[4] * o[1] - h - SIN9[1] * o[3]
    three = ROOT3H * (o[0] - o[1] + o[3])
    four = SIN9[4] * o[0] - SIN9[1] * o[1] + h - SIN9[2] * o[3]
    return [one, two, three, four]


def real9(y):
    e = [y[m] + y[9 - m] for m in range(1, 5)]
    o = [y[m] - y[9 - m] for m in range(1, 5)]
    s = sin_sums(o)
    return cos_sums(y[0], e), [None] + [-v for v in s]


def forward36(x):
    y0, y2, y1r, y1i = [], [], [], []
    for b2 in range(9):
        x0, x1, x2, x3 = (x[(9 * b1 + 4 * b2) % 36] for b1 in range(4))
        u0, u1, v0, v1 = x0 + x2, x0 - x2, x1 + x3, x3 - x1
        y0.append(u0 + v0)
        y2.append(u0 - v0)
        y1r.append(u1)
        y1i.append(v1)
    z0r, z0i = real9(y0)
    z2r, z2i = real9(y2)
    ur, ui = real9(y1r)
    vr, vi = real9(y1i)
    z1r, z1i = [None] * 9, [None] * 9
    z1r[0], z1i[0] = ur[0], vr[0]
    for f in range(1, 5):
        z1r[f], z1i[f] = ur[f] - vi[f], ui[f] + vr[f]
        z1r[9 - f], z1i[9 - f] = ur[f] + vi[f], vr[f] - ui[f]

    def at(f):
        f1, f2 = f % 4, f % 9
        if f1 in (0, 2):
            r, i = (z0r, z0i) if f1 == 0 else (z2r, z2i)
            if f2 == 0:
                return r[0], None
            return (r[f2], i[f2]) if f2 <= 4 else (r[9 - f2], -i[9 - f2])
        if f1 == 1:
            return z1r[f2], z1i[f2]
        g = (9 - f2) % 9
        return z1r[g], -z1i[g]

    return [(at(0)[0], at(18)[0])] + [at(f) for f in range(1, HALF)]


def inverse36(pairs):
    def spec(f):
        f %= 36
        if f == 0:
            return pairs[0][0], None
        if f == 18:
            return pairs[0][1], None
        if f < 18:
            return pairs[f]
        r, i = pairs[36 - f]
        return r, -i

    def find(f1, f2):
        return spec(next(f for f in range(36) if f % 4 == f1 and f % 9 == f2))

    def hermitian(f1):
        r0 = find(f1, 0)[0]
        z = [find(f1, f) for f in range(1, 5)]
        c = cos_sums(r0, [2.0 * r for r, _ in z])
        s = sin_sums([2.0 * i for _, i in z])
        y = [None] * 9
        y[0] = c[0]
        for m in range(1, 5):
            y[m], y[9 - m] = c[m] - s[m - 1], c[m] + s[m - 1]
        return y

    y0, y2 = hermitian(0), hermitian(2)
    z = [find(1, f) for f in range(9)]
    er = [z[f][0] + z[9 - f][0] for f in range(1, 5)]
    ei = [z[f][1] + z[9 - f][1] for f in range(1, 5)]
    dr = [z[f][0] - z[9 - f][0] for f in range(1, 5)]
    di = [z[f][1] - z[9 - f][1] for f in range(1, 5)]
    cr, ci = cos_sums(z[0][0], er), cos_sums(z[0][1], ei)
    sr, si = sin_sums(dr), sin_sums(di)
    y1r, y1i = [cr[0]] + [None] * 8, [ci[0]] + [None] * 8
    for m in range(1, 5):
        y1r[m], y1r[9 - m] = cr[m] - si[m - 1], cr[m] + si[m - 1]
        y1i[m], y1i[9 - m] = ci[m] + sr[m - 1], ci[m] - sr[m - 1]
    x = [None] * 36
    for b2 in range(9):
        p, q = y0[b2] + y2[b2], y0[b2] - y2[b2]
        a, b = 2.0 * y1r[b2], 2.0 * y1i[b2]
        for b1, v in enumerate((p + a, q - b, p - a, q + b)):
            x[(9 * b1 + 4 * b2) % 36] = v
    return x


def lane(shape):
    return lax.broadcasted_iota(jnp.int32, shape, len(shape) - 1)


def turn32(a):
    l = lane(a[0].shape)
    low = l < 64
    even = (l // 32) % 2 == 0
    b0 = jnp.where(low, a[0], pltpu.roll(a[2], 64, 1))
    b2 = jnp.where(low, pltpu.roll(a[0], 64, 1), a[2])
    b1 = jnp.where(low, a[1], pltpu.roll(a[3], 64, 1))
    b3 = jnp.where(low, pltpu.roll(a[1], 64, 1), a[3])
    out = []
    for p, q in ((b0, b1), (b2, b3)):
        out.append(jnp.where(even, p, pltpu.roll(q, 32, 1)))
        out.append(jnp.where(even, pltpu.roll(p, 96, 1), q))
    return out


def split(v):
    h = v.astype(BF16)
    return h, (v - h.astype(F32)).astype(BF16)


NT = (((1,), (1,)), ((), ()))
NN = (((1,), (0,)), ((), ()))


def dot(a, b, dims=NN):
    return lax.dot_general(a, b, dims, preferred_element_type=F32)


def kernel(
    prior, images, refs, perm, out,
    rows16, tload, x5, xh, tbuf, tf, tmix, offs, sh, stat, lh, mass, cf, cmix, cb, rb,
    load_sem, perm_sem, send_sem, recv_sem, off_send, off_recv, pair_send, pair_recv, rs_send, rs_recv,
):
    img, ref = lax.axis_index("img"), lax.axis_index("ref")
    z, yh = img // 2, img % 2
    x, yl, core = ref // 4, (ref // 2) % 2, ref % 2

    def dev(x_, y_, z_, c_):
        return {"img": z_ * 2 + y_ // 2, "ref": x_ * 4 + (y_ % 2) * 2 + c_}

    y = yh * 2 + yl
    xp, xm = (x + 1) % 4, (x + 3) % 4
    x2 = (x + 2) % 4
    to_xp, to_xm = dev(xp, y, z, core), dev(xm, y, z, core)
    to_yp, to_ym = dev(x, (y + 1) % 4, z, core), dev(x, (y + 3) % 4, z, core)
    sibling = dev(x, y, z, 1 - core)

    loads = []
    for k in range(12):
        c = pltpu.make_async_copy(refs.at[pl.ds(36 * k // 16 * 16, 16)], rows16.at[k], load_sem.at[k])
        c.start()
        loads.append(c)

    def away(d):
        zz, hh, xx, ll = d // 16, (d // 8) % 2, (d // 2) % 4, d % 2
        return {
            "img": ((z + zz) % 4) * 2 + (yh + hh) % 2,
            "ref": ((x + xx) % 4) * 4 + ((yl + ll) % 2) * 2 + core,
        }

    barrier = pltpu.get_barrier_semaphore()

    def greet(d, c):
        pl.semaphore_signal(barrier, inc=1, device_id=away(d), device_id_type=MESH)
        return c

    lax.fori_loop(1, 64, greet, 0)
    pl.semaphore_signal(barrier, inc=1, device_id=sibling, device_id_type=MESH)
    pl.semaphore_wait(barrier, 64)

    for c in loads:
        c.wait()
    norm = jnp.zeros((16, 128), F32)
    for g in range(8):
        tiles = []
        for k in range(12):
            at = 36 * k % 16
            tiles.append(rows16[k, :, g * BAND : (g + 1) * BAND].astype(F32)[at : at + 1])
        tiles.append(jnp.zeros((4, BAND), F32))
        t = jnp.concatenate(tiles, axis=0)
        for v in range(9):
            part = t[:, v * 128 : (v + 1) * 128]
            norm = norm + part * part
        tload[g * 16 : (g + 1) * 16, :] = t.astype(BF16)
    half_norm = 0.5 * jnp.sum(norm, axis=1, keepdims=True)
    rowid = lax.broadcasted_iota(jnp.int32, (16, 128), 0)
    pri = jnp.ones((16, 128), F32)
    for k in range(12):
        pri = jnp.where(rowid == k, prior[k], pri)
    slot = x * 2 + yl
    offs[slot] = jnp.log(pri) - half_norm

    sub8 = lax.broadcasted_iota(jnp.int32, (8, 128), 0)

    def arrange(v, c):
        o = dot(tload[...], perm[:, pl.ds(pl.multiple_of(v * 128, 128), 128)])
        halves = [turn32([o[(2 * zz + h) * 16 : (2 * zz + h) * 16 + 16] for zz in range(4)]) for h in range(2)]
        rows = []
        for i in range(4):
            a, b = halves[0][i], halves[1][i]
            rows += [a[:8], b[:8], jnp.where(sub8 < 4, a[8:], pltpu.roll(b[8:], 4, 0))]
        tbuf[slot, pl.ds(pl.multiple_of(96 * v, 32), 96), :] = jnp.concatenate(rows, axis=0).astype(BF16)
        return c

    lax.fori_loop(0, 9, arrange, 0)

    def piece(s, half):
        return tbuf.at[s, pl.ds(432 * half, 432)]

    started = []

    def send(s, half, target, n):
        c = pltpu.make_async_remote_copy(
            piece(s, half), piece(s, half), send_sem.at[n], recv_sem.at[n], device_id=target, device_id_type=MESH
        )
        c.start()
        started.append(c)

    def arrived(s, half, n):
        pltpu.make_async_copy(piece(s, half), piece(s, half), recv_sem.at[n]).wait()

    send(slot, 0, to_xp, 0)
    send(slot, 1, to_xm, 2)
    send(slot, 0, to_yp, 6)
    send(slot, 1, to_ym, 7)
    send(slot, 1, to_xp, 1)
    send(slot, 0, to_xm, 3)
    off_copies = []
    for d in range(1, 8):
        c = pltpu.make_async_remote_copy(
            offs.at[slot], offs.at[slot], off_send.at[d], off_recv.at[d], device_id=away(d), device_id_type=MESH
        )
        c.start()
        off_copies.append(c)
    s_m, s_p, s_2 = xm * 2 + yl, xp * 2 + yl, x2 * 2 + yl
    o_0, o_m, o_p, o_2 = x * 2 + 1 - yl, xm * 2 + 1 - yl, xp * 2 + 1 - yl, x2 * 2 + 1 - yl

    for g in range(3):
        cols = slice(g * 384, g * 384 + 384)
        parts = [dot(images[:, q * BAND : (q + 1) * BAND], perm[:, cols]) for q in range(8)]
        for vv in range(3):
            v = 3 * g + vv
            for h in range(2):
                t = turn32([parts[2 * zz + h][:, vv * 128 : vv * 128 + 128] for zz in range(4)])
                for i in range(4):
                    x5[core, 4 * v + i, :, h * 128 : h * 128 + 128] = t[i].astype(BF16)
    swap = pltpu.make_async_remote_copy(
        x5.at[core], x5.at[core], pair_send.at[0], pair_recv.at[0], device_id=sibling, device_id_type=MESH
    )
    swap.start()

    arrived(s_m, 0, 0)
    send(s_m, 0, to_xp, 4)
    send(s_m, 0, to_yp, 8)
    arrived(s_p, 1, 2)
    send(s_p, 1, to_xm, 5)
    send(s_p, 1, to_ym, 9)

    def image_spectra(c):
        def step(n, carry):
            t, h = n // 2, n % 2
            r0 = pl.multiple_of(t * 16, 16)
            lanes = pl.ds(pl.multiple_of(h * 128, 128), 128)
            p = forward36([x5[c, b, pl.ds(r0, 16), lanes].astype(F32) for b in range(36)])
            for f in range(HALF):
                for ri in range(2):
                    a, b = split(p[f][ri])
                    at = pl.ds(pl.multiple_of(ri * 128 + c * 64 + r0, 16), 16)
                    xh[f, 0, at, lanes] = a
                    xh[f, 1, at, lanes] = b
            return carry

        lax.fori_loop(0, 8, step, 0)

    image_spectra(core)
    arrived(s_p, 0, 3)
    send(s_p, 0, to_yp, 10)
    arrived(s_m, 1, 1)
    send(s_m, 1, to_ym, 11)
    swap.wait()
    image_spectra(1 - core)
    arrived(s_2, 0, 4)
    send(s_2, 0, to_yp, 12)
    arrived(s_2, 1, 5)
    send(s_2, 1, to_ym, 13)

    def template_spectra(xx, ll):
        s = xx * 2 + ll
        raw = []
        for b in range(HALF):
            two = tbuf[s, 48 * b : 48 * b + 48, :].astype(F32)
            raw += [two[:24], two[24:]]
        p = forward36(raw)
        at = pl.ds(pl.multiple_of(ll * 32 + xx * 8, 8), 8)
        for f in range(HALF):
            for ri in range(2):
                v = p[f][ri]
                tf[f, ri, at, 0:128] = v[0:8]
                tf[f, ri, at, 128:256] = v[8:16]
                tmix[s, f, ri] = v[16:24]

    def own_row(n, c):
        template_spectra((x + n) % 4, yl)
        return c

    lax.fori_loop(0, 4, own_row, 0)
    arrived(o_0, 0, 6)
    arrived(o_0, 1, 7)
    arrived(o_m, 0, 8)
    arrived(o_p, 1, 9)
    arrived(o_p, 0, 10)
    arrived(o_m, 1, 11)
    arrived(o_2, 0, 12)
    arrived(o_2, 1, 13)

    def other_row(n, c):
        template_spectra((x + n) % 4, 1 - yl)
        return c

    lax.fori_loop(0, 4, other_row, 0)
    for c in off_copies:
        c.wait()

    def score(f, c):
        for ri in range(2):
            mix = [tmix[s, f, ri] for s in range(8)]
            for xx in range(4):
                a, b = mix[2 * xx], mix[2 * xx + 1]
                tf[f, ri, 64 + 8 * xx : 72 + 8 * xx, 0:128] = jnp.where(sub8 < 4, a, pltpu.roll(b, 4, 0))
                tf[f, ri, 64 + 8 * xx : 72 + 8 * xx, 128:256] = jnp.where(sub8 < 4, pltpu.roll(a, 4, 0), b)
        rh, rl = split(tf[f, 0])
        ih, il = split(tf[f, 1])
        high = jnp.concatenate([rh, ih], axis=0)
        low = jnp.concatenate([rl, il], axis=0)
        m = dot(high, xh[f, 0], NT) + (dot(low, xh[f, 0], NT) + dot(high, xh[f, 1], NT))
        rr, ri_, ir, ii = m[:96, :128], m[:96, 128:], m[96:, :128], m[96:, 128:]
        first = f == 0
        sh[2 * f] = jnp.where(first, rr, rr + ii)
        sh[2 * f + 1] = jnp.where(first, ii, ri_ - ir)
        return c

    lax.fori_loop(0, HALF, score, 0)

    def to_turns(xx, off, rows, top):
        p = [(sh[2 * f, rows, :], sh[2 * f + 1, rows, :]) for f in range(HALF)]
        s = inverse36(p)
        for r in range(36):
            v = s[r] * (1.0 / 36.0) + off
            sh[r, rows, :] = v
            top = jnp.maximum(top, v)
        return top

    def rows_of(n, c):
        lo, hi = n % 4, n // 4
        plain = offs[lo * 2 + jnp.minimum(hi, 1)]
        a, b = offs[lo * 2], offs[lo * 2 + 1]
        last = jnp.where(sub8 < 4, a[8:], pltpu.roll(b[8:], 4, 0))
        off = jnp.where(hi == 2, last, plain[:8])
        return to_turns(lo, off, pl.ds(pl.multiple_of(n * 8, 8), 8), c)

    top8 = lax.fori_loop(0, 12, rows_of, jnp.full((8, 128), -jnp.inf, F32))
    top = jnp.max(top8, axis=0, keepdims=True)

    def raise_(n, c):
        rows = pl.ds(pl.multiple_of(n * 8, 8), 8)
        for r in range(36):
            e = jnp.exp(sh[r, rows, :] - top)
            sh[r, rows, :] = e
            c = c + e
        return c

    total = jnp.sum(lax.fori_loop(0, 12, raise_, jnp.zeros((8, 128), F32)), axis=0, keepdims=True)
    stat[0, 0] = jnp.broadcast_to(top, (8, 128))
    stat[0, 1] = jnp.broadcast_to(total, (8, 128))
    share = pltpu.make_async_remote_copy(
        stat.at[0], stat.at[1], pair_send.at[1], pair_recv.at[1], device_id=sibling, device_id_type=MESH
    )
    share.start()
    share.wait()
    top_o, total_o = stat[1, 0][:1], stat[1, 1][:1]
    peak = jnp.maximum(top, top_o)
    mine = jnp.exp(top - peak)
    scale = mine / (total * mine + total_o * jnp.exp(top_o - peak))

    def weigh(n, c):
        rows = pl.ds(pl.multiple_of(n * 16, 16), 16)
        upper = pl.ds(pl.multiple_of(n * 16 + 96, 16), 16)
        w = [(sh[r, rows, :] * scale).astype(BF16).astype(F32) for r in range(36)]
        p = forward36(w)
        mass[rows, :] = jnp.broadcast_to(jnp.sum(p[0][0], axis=1, keepdims=True), (16, 128))
        none = jnp.zeros((16, 128), BF16)
        for f in range(HALF):
            for part, (r, i) in enumerate(zip(split(p[f][0]), split(p[f][1]))):
                lh[f, part, rows, 0:128] = r
                lh[f, part, rows, 128:256] = none if f == 0 else i
                lh[f, part, upper, 0:128] = none if f == 0 else -i
                lh[f, part, upper, 128:256] = i if f == 0 else r
        return c

    lax.fori_loop(0, 6, weigh, 0)

    def sums(u, c):
        comps = []
        for ff in range(2):
            f = 2 * u + ff
            a, b = lh[f, 0], lh[f, 1]
            m = dot(a, xh[f, 0]) + (dot(b, xh[f, 0]) + dot(a, xh[f, 1]))
            comps += [m[:96], m[96:]]
        at = pl.ds(pl.multiple_of(8 * u, 8), 8)
        for h in range(2):
            t = turn32([v[:, h * 128 : h * 128 + 128] for v in comps])
            for zz in range(4):
                for xx in range(4):
                    cf[zz, h, xx, 0, at, :] = t[zz][8 * xx : 8 * xx + 8]
                    cf[zz, h, xx, 1, at, :] = t[zz][32 + 8 * xx : 40 + 8 * xx]
                    cmix[zz, h, xx, u] = t[zz][64 + 8 * xx : 72 + 8 * xx]
        return c

    lax.fori_loop(0, 9, sums, 0)

    l8 = lane((8, 128)) // 16

    def pack(zz, hh, xx):
        mixes = [cmix[zz, hh, xx, u] for u in range(9)]
        tail0, tail1 = [], []
        for u in range(0, 8, 2):
            a, b = mixes[u], mixes[u + 1]
            tail0.append(jnp.where(sub8 < 4, a, pltpu.roll(b, 4, 0)))
            tail1.append(jnp.where(sub8 < 4, pltpu.roll(a, 4, 0), b))
        mm = mass[pl.ds(pl.multiple_of(64 + 8 * xx, 8), 8), :]
        m0 = mass[pl.ds(pl.multiple_of(8 * xx, 8), 8), :]
        m1 = mass[pl.ds(pl.multiple_of(32 + 8 * xx, 8), 8), :]
        for ll, (m8, m4, last) in enumerate(
            ((m0, pltpu.roll(mm, 4, 0), mixes[8]), (m1, mm, pltpu.roll(mixes[8], 4, 0)))
        ):
            v = jnp.where(l8 < 2, pltpu.roll(m8, 4, 0), jnp.where(l8 < 4, m8, m4))
            vh = v.astype(BF16).astype(F32)
            v = jnp.where(l8 % 2 == 0, vh, v - vh)
            (tail0, tail1)[ll].append(jnp.where(sub8 < 4, last, v))
        for ll, tail in enumerate((tail0, tail1)):
            cb[zz, hh, xx, ll] = jnp.concatenate(
                [cf[zz, hh, xx, ll, 0:72, :]] + tail, axis=0
            ).astype(BF16)

    def pack_step(n, c):
        pack(n // 8, (n // 4) % 2, n % 4)
        return c

    lax.fori_loop(0, 32, pack_step, 0)

    def scatter_copy(d):
        zz, hh, xx, ll = (z + d // 16) % 4, (yh + d // 8) % 2, (x + (d // 2) % 4) % 4, (yl + d) % 2
        return pltpu.make_async_remote_copy(
            cb.at[zz, hh, xx, ll], rb.at[d], rs_send.at[d], rs_recv.at[d], device_id=away(d), device_id_type=MESH
        )

    def scatter(d, c):
        scatter_copy(d).start()
        return c

    lax.fori_loop(1, 64, scatter, 0)
    acc = cb[z, yh, x, yl].astype(F32)

    def gather(d, acc):
        scatter_copy(d).wait_recv()
        return acc + rb[d].astype(F32)

    out[...] = lax.fori_loop(1, 64, gather, acc)

    def finish(d, c):
        scatter_copy(d).wait_send()
        return c

    lax.fori_loop(1, 64, finish, 0)
    for c in started:
        c.wait_send()


def column_order():
    q, b, c = np.meshgrid(np.arange(8), np.arange(ROT), np.arange(TURN), indexing="ij")
    perm = np.zeros((BAND, BAND), np.float32)
    perm[(q * ANG + b * TURN + c).ravel(), (b * 32 + q * 4 + c).ravel()] = 1
    return perm


def real_idft():
    b = np.arange(ROT)
    rows = [np.ones(ROT) / ROT, (-1.0) ** b / ROT]
    for f in range(1, HALF):
        rows.append(2 * np.cos(2 * np.pi * f * b / ROT) / ROT)
        rows.append(-2 * np.sin(2 * np.pi * f * b / ROT) / ROT)
    return np.array(rows).astype(np.float32).reshape(9, 4, ROT)


def per_device(images, references, class_prior):
    perm = jnp.asarray(column_order(), BF16)
    vmem = pl.BlockSpec(memory_space=pltpu.VMEM)
    v = pl.pallas_call(
        kernel,
        out_shape=jax.ShapeDtypeStruct((112, 128), F32),
        in_specs=[
            pl.BlockSpec(memory_space=pltpu.SMEM),
            vmem,
            pl.BlockSpec(memory_space=pl.ANY),
            vmem,
        ],
        out_specs=vmem,
        scratch_shapes=[
            pltpu.VMEM((12, 16, 9216), BF16),
            pltpu.VMEM((128, BAND), BF16),
            pltpu.VMEM((2, 36, 64, 256), BF16),
            pltpu.VMEM((HALF, 2, 256, 256), BF16),
            pltpu.VMEM((8, 864, 128), BF16),
            pltpu.VMEM((HALF, 2, 96, 256), F32),
            pltpu.VMEM((8, HALF, 2, 8, 128), F32),
            pltpu.VMEM((8, 16, 128), F32),
            pltpu.VMEM((36, 96, 128), F32),
            pltpu.VMEM((2, 2, 8, 128), F32),
            pltpu.VMEM((HALF, 2, 192, 256), BF16),
            pltpu.VMEM((96, 128), F32),
            pltpu.VMEM((4, 2, 4, 2, 72, 128), F32),
            pltpu.VMEM((4, 2, 4, 9, 8, 128), F32),
            pltpu.VMEM((4, 2, 4, 2, 112, 128), BF16),
            pltpu.VMEM((64, 112, 128), BF16),
            pltpu.SemaphoreType.DMA((12,)),
            pltpu.SemaphoreType.DMA((1,)),
            pltpu.SemaphoreType.DMA((14,)),
            pltpu.SemaphoreType.DMA((14,)),
            pltpu.SemaphoreType.DMA((8,)),
            pltpu.SemaphoreType.DMA((8,)),
            pltpu.SemaphoreType.DMA((2,)),
            pltpu.SemaphoreType.DMA((2,)),
            pltpu.SemaphoreType.DMA((64,)),
            pltpu.SemaphoreType.DMA((64,)),
        ],
        compiler_params=pltpu.CompilerParams(
            collective_id=0, has_side_effects=True, vmem_limit_bytes=56 * 1024 * 1024
        ),
        name="em_pass",
    )(class_prior, images, references, perm)
    low = v[:72].reshape(9, 8, 4, 8, TURN)
    high = v[72:108].reshape(9, 4, 4, 8, TURN)
    val = jnp.concatenate([low, high], axis=1)
    sums = jnp.einsum("ukiqc,uib->kqbc", val, real_idft(), precision=lax.Precision.HIGHEST)
    m = v[108:112].reshape(4, 8, 16)[:, :6, 0].reshape(4, 3, 2)
    class_weights = jnp.sum(m, axis=2).T.reshape(12)
    return (sums.reshape(12, BAND), class_weights)


def solution(mesh):
    placed = (P(("img", "ref"), None), P("ref", None), P("ref"))
    return jax.shard_map(
        per_device,
        mesh=mesh,
        in_specs=placed,
        out_specs=(P("ref", "img"), P("ref")),
        check_vma=False,
    )
```

time: 435 us -> 87.8 us (0.20)
  waiting for transfers between devices: 270 us -> 0 us
  blocking collectives: 82.2 us -> 0 us
  Pallas kernels: 0 us -> 78.2 us
  matrix products: 31.7 us -> 1.01 us
  local copies, waits for them, and re-layouts: 24.3 us -> 7.58 us
  between operations: 14.1 us -> 0.69 us
  other arithmetic: 11.7 us -> 0.02 us
    reduce_scatter x1 -> x0, waiting for transfers between devices: 169 us -> none  [per_device(): reduced = lax.psum_scatter(sums, 'img', scatter_dimension=1, tiled=True)]
    all_gather x1 -> x0, waiting for transfers between devices: 100 us -> none  [per_device(): gathered = lax.all_gather(images, 'ref', axis=0, tiled=True)]
    pallas_call x0 -> x1, Pallas kernels: none -> 78.2 us  [per_device(): pl.pallas_call(kernel, out_shape=jax.ShapeDtypeStruct((112, 128), F32), i...]
    psum x2 -> x0, blocking collectives: 52.4 us -> none  [the longest x1 27.1 us: per_device(): lax.psum(jnp.sum(jnp.exp(scores - top_score[:, None]), axis=1), 'ref')]
    dot_general x2 -> x1, matrix products: 31.7 us -> 1.01 us  [per_device(): jnp.einsum('ukiqc,uib->kqbc', val, real_idft(), precision=lax.Precision.H...]
    pmax x1 -> x0, blocking collectives: 29.8 us -> none  [per_device(): top_score = lax.pmax(local_max, 'ref')]
    squeeze x19 -> x0, local copies, waits for them, and re-layouts: 18.9 us -> none  [unturn(): result = result + doubled[:, turn_index, :, start_col:start_col + ANG]]
    reshape x1 -> x6, local copies, waits for them, and re-layouts: 0.08 us -> 5.42 us  [the longest x2 3.19 us: per_device(): low = v[:72].reshape(9, 8, 4, 8, TURN)]
  transfers between devices with their start and end apart: 2 -> 0, of which waited for: 2 -> 0; matrix products, arithmetic and copies ran while one was open for 1% -> 0% of each run, Pallas kernels for 0% -> 0%
where the time goes in v2:
time: 87.8 us; the launch traced here: 87.5 us
  Pallas kernels  78.2 us (89%)
  local copies, waits for them, and re-layouts  7.58 us (9%)
  matrix products  1.01 us (1%)
    pallas_call x1, Pallas kernels, per_device(): pl.pallas_call(kernel, out_shape=jax.ShapeDtypeStruct((112, 128), F32), i...  78.2 us
    reshape x2, local copies, waits for them, and re-layouts, per_device(): low = v[:72].reshape(9, 8, 4, 8, TURN)  3.19 us

profile of v2, /device:TPU:0, one launch (start us, length us, event | category | flops | bytes accessed | tf_op | source)
XLA Modules:
  0.0 87.5 jit_solution(17410258294528539591)
XLA Ops:
  0.6 78.2 %em_pass.1 = f32[112,128]{1,0:T(8,128)} custom-call(f32[12]{0:T(128)} %prior.1, bf16[64,9216]{1,0:T(8,128)(2,1)} %images.1, bf16[432,9216]{1,0:T(8,128)(2,1)} %refs.1, bf16[1152,1152]{1,0:T(8,128)(2,1)} %constant.6.clone.perm), custom_call_target="tpu_custom_call" | custom-call | tf_op jit(solution)/shard_map/em_pass/pallas_call | solution.py:533
  78.9 0.0 slice-start
  78.9 0.0 copy-start.1
  78.9 0.8 slice.12
  79.7 1.2 %reshape.26 = f32[9,8,4,8,4]{4,3,2,1,0:T(8,128)S(1)} reshape(f32[72,128]{1,0:T(8,128)S(1)} %slice.12) | data formatting | bytes 73728 | tf_op jit(solution)/shard_map/reshape | solution.py:576
  80.9 0.0 copy-start
  80.9 2.0 %copy.11 = f32[9,8,4,8,4]{0,1,2,4,3:T(8,128)S(1)} copy(f32[9,8,4,8,4]{4,3,2,1,0:T(8,128)S(1)} %reshape.26) | data formatting | bytes 73728 | tf_op jit(solution)/shard_map/reshape | solution.py:576
  82.9 0.0 slice-done
  82.9 0.6 reshape.20
  83.5 0.9 %copy.12 = f32[9,4,4,8,4]{0,1,2,4,3:T(4,128)S(1)} copy(f32[9,4,4,8,4]{4,3,2,1,0:T(8,128)S(1)} %reshape.20) | data formatting | bytes 36864 | tf_op jit(solution)/shard_map/reshape | solution.py:577
  84.4 0.0 copy-done.1
  84.4 1.0 %convolution_bitcast_fusion = f32[12,8,36,4]{2,0,3,1:T(8,128)S(1)} fusion(f32[9,4,36,1,1]{2,0,1,4,3:T(8,128)S(1)} %copy-done.1, f32[9,4,4,8,4]{0,1,2,4,3:T(4,128)S(1)} %copy.12, f32[9,8,4,8,4]{0,1,2,4,3:T(8,128)S(1)} %copy.11), kind=kOutput, calls=%fused_computation | convolution fusion | flops 5985792 | bytes 115776 | tf_op jit(solution)/shard_map/ukiqc,uib->kqbc/dot_general | solution.py:579
  85.4 0.3 copy.13
  85.8 0.9 copy.15
  86.7 0.0 copy-done
  86.7 0.1 reshape.22
  86.7 0.1 copy.20
  86.9 0.6 reshape.23
  (3 shorter events, 0.0 us)
Async XLA Ops:
  78.9 4.0 %slice-start = ((f32[112,128]{1,0:T(8,128)}), f32[36,128]{1,0:T(8,128)S(1)}, s32[]{:S(2)}) async-start(f32[112,128]{1,0:T(8,128)} %em_pass.1), calls=%async_computation | async-start | bytes 40960 | tf_op jit(solution)/shard_map/slice | solution.py:577
  78.9 5.6 %copy-start.1 = (f32[9,4,36,1,1]{2,0,1,4,3:T(8,128)S(1)}, f32[9,4,36,1,1]{2,0,1,4,3:T(8,128)}, u32[]{:S(2)}) copy-start(f32[9,4,36,1,1]{2,0,1,4,3:T(8,128)} %constant.10) | copy-start | bytes 15556
  80.9 5.8 %copy-start = (f32[112,128]{1,0:T(8,128)S(1)}, f32[112,128]{1,0:T(8,128)}, u32[]{:S(2)}) copy-start(f32[112,128]{1,0:T(8,128)} %em_pass.1) | copy-start | bytes 172036

commit v3 on v2

--- a/solution.py
+++ b/solution.py
@@ -162,9 +162,10 @@
 
 
 def kernel(
-    prior, images, refs, perm, out,
-    rows16, tload, x5, xh, tbuf, tf, tmix, offs, sh, stat, lh, mass, cf, cmix, cb, rb,
-    load_sem, perm_sem, send_sem, recv_sem, off_send, off_recv, pair_send, pair_recv, rs_send, rs_recv,
+    prior, images_hbm, refs, perm_hbm, out, out_mass,
+    images, perm, rows16, tload, x5, xh, tbuf, tf, tmix, offs, sh, stat, lh, mass, cf, cmix,
+    own_a, own_b, own_c, s1a, s1b, s1c, r1a, r1b, r1c, s2a, s2b, s2c, r2a, r2b, r2c, s3a, s3b, s3c, r3a, r3b, r3c,
+    load_sem, send_sem, recv_sem, off_send, off_recv, pair_send, pair_recv, rs_send, rs_recv,
 ):
     img, ref = lax.axis_index("img"), lax.axis_index("ref")
     z, yh = img // 2, img % 2
@@ -185,23 +186,23 @@
         c = pltpu.make_async_copy(refs.at[pl.ds(36 * k // 16 * 16, 16)], rows16.at[k], load_sem.at[k])
         c.start()
         loads.append(c)
+    load_perm = pltpu.make_async_copy(perm_hbm, perm, load_sem.at[12])
+    load_perm.start()
+    load_images = pltpu.make_async_copy(images_hbm, images, load_sem.at[13])
+    load_images.start()
+
+    def along(axis, r):
+        x_, y_, z_ = ((v + r * (a == axis)) % 4 for a, v in enumerate((x, y, z)))
+        return dev(x_, y_, z_, core)
 
     def away(d):
-        zz, hh, xx, ll = d // 16, (d // 8) % 2, (d // 2) % 4, d % 2
-        return {
-            "img": ((z + zz) % 4) * 2 + (yh + hh) % 2,
-            "ref": ((x + xx) % 4) * 4 + ((yl + ll) % 2) * 2 + core,
-        }
+        return dev((x + d // 2) % 4, yh * 2 + (yl + d) % 2, z, core)
 
     barrier = pltpu.get_barrier_semaphore()
-
-    def greet(d, c):
-        pl.semaphore_signal(barrier, inc=1, device_id=away(d), device_id_type=MESH)
-        return c
-
-    lax.fori_loop(1, 64, greet, 0)
-    pl.semaphore_signal(barrier, inc=1, device_id=sibling, device_id_type=MESH)
-    pl.semaphore_wait(barrier, 64)
+    partners = [along(a, r) for a in range(3) for r in range(1, 4)] + [away(d) for d in (3, 5, 7)] + [sibling]
+    for p in partners:
+        pl.semaphore_signal(barrier, inc=1, device_id=p, device_id_type=MESH)
+    pl.semaphore_wait(barrier, len(partners))
 
     for c in loads:
         c.wait()
@@ -227,6 +228,8 @@
 
     sub8 = lax.broadcasted_iota(jnp.int32, (8, 128), 0)
 
+    load_perm.wait()
+
     def arrange(v, c):
         o = dot(tload[...], perm[:, pl.ds(pl.multiple_of(v * 128, 128), 128)])
         halves = [turn32([o[(2 * zz + h) * 16 : (2 * zz + h) * 16 + 16] for zz in range(4)]) for h in range(2)]
@@ -237,7 +240,7 @@
         tbuf[slot, pl.ds(pl.multiple_of(96 * v, 32), 96), :] = jnp.concatenate(rows, axis=0).astype(BF16)
         return c
 
-    lax.fori_loop(0, 9, arrange, 0)
+    lax.fori_loop(0, 9, arrange, 0, unroll=9)
 
     def piece(s, half):
         return tbuf.at[s, pl.ds(432 * half, 432)]
@@ -270,9 +273,12 @@
     s_m, s_p, s_2 = xm * 2 + yl, xp * 2 + yl, x2 * 2 + yl
     o_0, o_m, o_p, o_2 = x * 2 + 1 - yl, xm * 2 + 1 - yl, xp * 2 + 1 - yl, x2 * 2 + 1 - yl
 
+    load_images.wait()
     for g in range(3):
         cols = slice(g * 384, g * 384 + 384)
-        parts = [dot(images[:, q * BAND : (q + 1) * BAND], perm[:, cols]) for q in range(8)]
+        stacked = jnp.concatenate([images[:, q * BAND : (q + 1) * BAND] for q in range(8)], axis=0)
+        o = dot(stacked, perm[:, cols])
+        parts = [o[q * 64 : q * 64 + 64] for q in range(8)]
         for vv in range(3):
             v = 3 * g + vv
             for h in range(2):
@@ -374,7 +380,7 @@
         sh[2 * f + 1] = jnp.where(first, ii, ri_ - ir)
         return c
 
-    lax.fori_loop(0, HALF, score, 0)
+    lax.fori_loop(0, HALF, score, 0, unroll=6)
 
     def to_turns(xx, off, rows, top):
         p = [(sh[2 * f, rows, :], sh[2 * f + 1, rows, :]) for f in range(HALF)]
@@ -451,17 +457,44 @@
                     cmix[zz, h, xx, u] = t[zz][64 + 8 * xx : 72 + 8 * xx]
         return c
 
-    lax.fori_loop(0, 9, sums, 0)
+    place = (x, y, z)
+    copies = []
+
+    def stage(n, axis, src, dst):
+        group = []
+        for r in range(1, 4):
+            c = pltpu.make_async_remote_copy(
+                src.at[(place[axis] + r) % 4], dst.at[r],
+                rs_send.at[3 * n + r - 1], rs_recv.at[3 * n + r - 1],
+                device_id=along(axis, r), device_id_type=MESH,
+            )
+            c.start()
+            group.append(c)
+            copies.append(c)
+        return group
+
+    def landed(group):
+        for c in group:
+            c.wait_recv()
+
+    def rows_a(zz, hh, xx, ll):
+        return cf[zz, hh, xx, ll, 0:48, :]
+
+    def pack_a(n, c):
+        zz, hh, xx = n // 8, (n // 4) % 2, n % 4
+        for ll in range(2):
+            s1a[xx, 2 * hh + ll, zz] = rows_a(zz, hh, xx, ll).astype(BF16)
+        return c
 
     l8 = lane((8, 128)) // 16
 
-    def pack(zz, hh, xx):
+    def rows_bc(zz, hh, xx):
         mixes = [cmix[zz, hh, xx, u] for u in range(9)]
-        tail0, tail1 = [], []
+        tails = ([], [])
         for u in range(0, 8, 2):
             a, b = mixes[u], mixes[u + 1]
-            tail0.append(jnp.where(sub8 < 4, a, pltpu.roll(b, 4, 0)))
-            tail1.append(jnp.where(sub8 < 4, pltpu.roll(a, 4, 0), b))
+            tails[0].append(jnp.where(sub8 < 4, a, pltpu.roll(b, 4, 0)))
+            tails[1].append(jnp.where(sub8 < 4, pltpu.roll(a, 4, 0), b))
         mm = mass[pl.ds(pl.multiple_of(64 + 8 * xx, 8), 8), :]
         m0 = mass[pl.ds(pl.multiple_of(8 * xx, 8), 8), :]
         m1 = mass[pl.ds(pl.multiple_of(32 + 8 * xx, 8), 8), :]
@@ -471,42 +504,116 @@
             v = jnp.where(l8 < 2, pltpu.roll(m8, 4, 0), jnp.where(l8 < 4, m8, m4))
             vh = v.astype(BF16).astype(F32)
             v = jnp.where(l8 % 2 == 0, vh, v - vh)
-            (tail0, tail1)[ll].append(jnp.where(sub8 < 4, last, v))
-        for ll, tail in enumerate((tail0, tail1)):
-            cb[zz, hh, xx, ll] = jnp.concatenate(
-                [cf[zz, hh, xx, ll, 0:72, :]] + tail, axis=0
-            ).astype(BF16)
-
-    def pack_step(n, c):
-        pack(n // 8, (n // 4) % 2, n % 4)
-        return c
-
-    lax.fori_loop(0, 32, pack_step, 0)
-
-    def scatter_copy(d):
-        zz, hh, xx, ll = (z + d // 16) % 4, (yh + d // 8) % 2, (x + (d // 2) % 4) % 4, (yl + d) % 2
-        return pltpu.make_async_remote_copy(
-            cb.at[zz, hh, xx, ll], rb.at[d], rs_send.at[d], rs_recv.at[d], device_id=away(d), device_id_type=MESH
-        )
-
-    def scatter(d, c):
-        scatter_copy(d).start()
-        return c
-
-    lax.fori_loop(1, 64, scatter, 0)
-    acc = cb[z, yh, x, yl].astype(F32)
-
-    def gather(d, acc):
-        scatter_copy(d).wait_recv()
-        return acc + rb[d].astype(F32)
-
-    out[...] = lax.fori_loop(1, 64, gather, acc)
-
-    def finish(d, c):
-        scatter_copy(d).wait_send()
-        return c
-
-    lax.fori_loop(1, 64, finish, 0)
+            tails[ll].append(jnp.where(sub8 < 4, last, v))
+        return [
+            (
+                jnp.concatenate([cf[zz, hh, xx, ll, 48:72, :], tails[ll][0]], axis=0),
+                jnp.concatenate(tails[ll][1:], axis=0),
+            )
+            for ll in range(2)
+        ]
+
+    def pack_bc(n, c):
+        zz, hh, xx = n // 8, (n // 4) % 2, n % 4
+        for ll, (b, c_) in enumerate(rows_bc(zz, hh, xx)):
+            s1b[2 * hh + ll, zz, xx] = b.astype(BF16)
+            s1c[zz, xx, 2 * hh + ll] = c_.astype(BF16)
+        return c
+
+    lax.fori_loop(0, 6, sums, 0, unroll=3)
+    lax.fori_loop(0, 32, pack_a, 0)
+    g1a = stage(0, 0, s1a, r1a)
+    lax.fori_loop(6, 9, sums, 0, unroll=3)
+    lax.fori_loop(0, 32, pack_bc, 0)
+    g1b = stage(1, 1, s1b, r1b)
+    g1c = stage(2, 2, s1c, r1c)
+
+    def keep_a(n, c):
+        for ll in range(2):
+            own_a[2 * (n % 2) + ll, n // 2] = rows_a(n // 2, n % 2, x, ll)
+        return c
+
+    def keep_b(n, c):
+        both = rows_bc(n // 4, yh, n % 4)
+        own_b[n // 4, n % 4] = jnp.where(yl == 0, both[0][0], both[1][0])
+        return c
+
+    def keep_c(n, c):
+        for ll, (_, v) in enumerate(rows_bc(z, n // 4, n % 4)):
+            own_c[n % 4, 2 * (n // 4) + ll] = v
+        return c
+
+    lax.fori_loop(0, 8, keep_a, 0)
+    lax.fori_loop(0, 16, keep_b, 0)
+    lax.fori_loop(0, 8, keep_c, 0)
+
+    def add_first(own, got, to):
+        def step(n, c):
+            i, j = n // 4, n % 4
+            to[i, j] = own[i, j] + (got[1, i, j].astype(F32) + got[2, i, j].astype(F32)) + got[3, i, j].astype(F32)
+            return c
+
+        lax.fori_loop(0, 16, step, 0)
+
+    def add_second(held, got, to, axis):
+        for j in range(4):
+            to[j] = held[place[axis], j] + (got[1, j] + got[2, j]) + got[3, j]
+
+    def add_third(held, got, axis):
+        return held[place[axis]] + (got[1] + got[2]) + got[3]
+
+    landed(g1a)
+    add_first(own_a, r1a, s2a)
+    g2a = stage(3, 1, s2a, r2a)
+    landed(g1b)
+    add_first(own_b, r1b, s2b)
+    g2b = stage(4, 2, s2b, r2b)
+    landed(g1c)
+    add_first(own_c, r1c, s2c)
+    g2c = stage(5, 0, s2c, r2c)
+    landed(g2a)
+    add_second(s2a, r2a, s3a, 1)
+    g3a = stage(6, 2, s3a, r3a)
+    landed(g2b)
+    add_second(s2b, r2b, s3b, 2)
+    g3b = stage(7, 0, s3b, r3b)
+    landed(g2c)
+    add_second(s2c, r2c, s3c, 0)
+    g3c = stage(8, 1, s3c, r3c)
+    landed(g3a)
+    part_a = add_third(s3a, r3a, 2)
+    landed(g3b)
+    part_b = add_third(s3b, r3b, 0)
+    landed(g3c)
+    part_c = add_third(s3c, r3c, 1)
+
+    v = jnp.concatenate([part_a, part_b, part_c], axis=0)
+    pairs = []
+    for u in range(9):
+        tail = v[72 + 8 * (u // 2) : 80 + 8 * (u // 2)]
+        if u % 2:
+            tail = pltpu.roll(tail, 4, 0)
+        both = jnp.concatenate([v[8 * u : 8 * u + 8], tail], axis=0)
+        comps = [both] + [pltpu.roll(both, 128 - 32 * i, 1) for i in range(1, 4)]
+        pairs += [(comps[0], comps[1]), (comps[2], comps[3])]
+    s = [w * (1.0 / 36.0) for w in inverse36(pairs)]
+    block = lane((16, 128)) // 32
+    cols = []
+    for b in range(0, 36, 4):
+        w = s[b]
+        for i in range(1, 4):
+            w = jnp.where(block == i, pltpu.roll(s[b + i], 32 * i, 1), w)
+        cols.append(w)
+    high, low = split(jnp.concatenate(cols, axis=1))
+    o = dot(jnp.concatenate([high, low], axis=0), perm[...], NT)
+    out[...] = (o[:16] + o[16:])[:12]
+    m = v[104:112]
+    m = m + pltpu.roll(m, 112, 1)
+    l128 = lane((8, 128))
+    for k in range(12):
+        out_mass[k] = jnp.sum(jnp.where((sub8 == 4 + k % 4) & (l128 == 32 * (k // 4)), m, 0.0))
+    for c in copies:
+        c.wait_send()
     for c in started:
         c.wait_send()
 
@@ -518,29 +625,20 @@
     return perm
 
 
-def real_idft():
-    b = np.arange(ROT)
-    rows = [np.ones(ROT) / ROT, (-1.0) ** b / ROT]
-    for f in range(1, HALF):
-        rows.append(2 * np.cos(2 * np.pi * f * b / ROT) / ROT)
-        rows.append(-2 * np.sin(2 * np.pi * f * b / ROT) / ROT)
-    return np.array(rows).astype(np.float32).reshape(9, 4, ROT)
-
-
 def per_device(images, references, class_prior):
     perm = jnp.asarray(column_order(), BF16)
     vmem = pl.BlockSpec(memory_space=pltpu.VMEM)
-    v = pl.pallas_call(
+    hbm = pl.BlockSpec(memory_space=pl.ANY)
+    smem = pl.BlockSpec(memory_space=pltpu.SMEM)
+    rows = (48, 32, 32)
+    return pl.pallas_call(
         kernel,
-        out_shape=jax.ShapeDtypeStruct((112, 128), F32),
-        in_specs=[
-            pl.BlockSpec(memory_space=pltpu.SMEM),
-            vmem,
-            pl.BlockSpec(memory_space=pl.ANY),
-            vmem,
-        ],
-        out_specs=vmem,
+        out_shape=(jax.ShapeDtypeStruct((12, BAND), F32), jax.ShapeDtypeStruct((12,), F32)),
+        in_specs=[smem, hbm, hbm, hbm],
+        out_specs=(pl.BlockSpec(memory_space=pltpu.VMEM), smem),
         scratch_shapes=[
+            pltpu.VMEM((64, 9216), BF16),
+            pltpu.VMEM((BAND, BAND), BF16),
             pltpu.VMEM((12, 16, 9216), BF16),
             pltpu.VMEM((128, BAND), BF16),
             pltpu.VMEM((2, 36, 64, 256), BF16),
@@ -555,31 +653,28 @@
             pltpu.VMEM((96, 128), F32),
             pltpu.VMEM((4, 2, 4, 2, 72, 128), F32),
             pltpu.VMEM((4, 2, 4, 9, 8, 128), F32),
-            pltpu.VMEM((4, 2, 4, 2, 112, 128), BF16),
-            pltpu.VMEM((64, 112, 128), BF16),
-            pltpu.SemaphoreType.DMA((12,)),
-            pltpu.SemaphoreType.DMA((1,)),
+            *[pltpu.VMEM((4, 4, r, 128), F32) for r in rows],
+            *[pltpu.VMEM((4, 4, 4, r, 128), BF16) for r in rows],
+            *[pltpu.VMEM((4, 4, 4, r, 128), BF16) for r in rows],
+            *[pltpu.VMEM((4, 4, r, 128), F32) for r in rows],
+            *[pltpu.VMEM((4, 4, r, 128), F32) for r in rows],
+            *[pltpu.VMEM((4, r, 128), F32) for r in rows],
+            *[pltpu.VMEM((4, r, 128), F32) for r in rows],
+            pltpu.SemaphoreType.DMA((14,)),
             pltpu.SemaphoreType.DMA((14,)),
             pltpu.SemaphoreType.DMA((14,)),
             pltpu.SemaphoreType.DMA((8,)),
             pltpu.SemaphoreType.DMA((8,)),
             pltpu.SemaphoreType.DMA((2,)),
             pltpu.SemaphoreType.DMA((2,)),
-            pltpu.SemaphoreType.DMA((64,)),
-            pltpu.SemaphoreType.DMA((64,)),
+            pltpu.SemaphoreType.DMA((27,)),
+            pltpu.SemaphoreType.DMA((27,)),
         ],
         compiler_params=pltpu.CompilerParams(
             collective_id=0, has_side_effects=True, vmem_limit_bytes=56 * 1024 * 1024
         ),
         name="em_pass",
     )(class_prior, images, references, perm)
-    low = v[:72].reshape(9, 8, 4, 8, TURN)
-    high = v[72:108].reshape(9, 4, 4, 8, TURN)
-    val = jnp.concatenate([low, high], axis=1)
-    sums = jnp.einsum("ukiqc,uib->kqbc", val, real_idft(), precision=lax.Precision.HIGHEST)
-    m = v[108:112].reshape(4, 8, 16)[:, :6, 0].reshape(4, 3, 2)
-    class_weights = jnp.sum(m, axis=2).T.reshape(12)
-    return (sums.reshape(12, BAND), class_weights)
 
 
 def solution(mesh):

time: 87.8 us -> 61.9 us (0.71)
  Pallas kernels: 78.2 us -> 58.4 us
  local copies, waits for them, and re-layouts: 7.58 us -> 2.63 us
  matrix products: 1.01 us -> 0 us
    pallas_call x1, Pallas kernels: 78.2 us -> 58.4 us  [per_device(): pl.pallas_call(kernel, out_shape=(jax.ShapeDtypeStruct((12, BAND), F32),...]
    reshape x6 -> x0, local copies, waits for them, and re-layouts: 5.42 us -> none  [the longest x2 3.19 us: per_device(): low = v[:72].reshape(9, 8, 4, 8, TURN)]
    unnamed x6 -> x2, local copies, waits for them, and re-layouts: 1.01 us -> 2.63 us
    dot_general x1 -> x0, matrix products: 1.01 us -> none  [per_device(): jnp.einsum('ukiqc,uib->kqbc', val, real_idft(), precision=lax.Precision.H...]
where the time goes in v3:
time: 61.9 us; the launch traced here: 61.7 us
  Pallas kernels  58.4 us (94%)
  local copies, waits for them, and re-layouts  2.63 us (4%)
  between operations  0.64 us (1%)
    pallas_call x1, Pallas kernels, per_device(): pl.pallas_call(kernel, out_shape=(jax.ShapeDtypeStruct((12, BAND), F32),...  58.4 us
    unnamed x2, local copies, waits for them, and re-layouts  2.63 us

profile of v3, /device:TPU:0, one launch (start us, length us, event | category | flops | bytes accessed | tf_op | source)
XLA Modules:
  0.0 61.7 jit_solution(18364133337171307867)
XLA Ops:
  0.6 58.4 %em_pass.1 = (f32[12,1152]{1,0:T(8,128)}, f32[12]{0:T(128)}) custom-call(f32[12]{0:T(128)} %prior.1, bf16[64,9216]{1,0:T(8,128)(2,1)} %images_hbm.1, bf16[432,9216]{1,0:T(8,128)(2,1)} %refs.1, bf16[1152,1152]{1,0:T(8,128)(2,1)} %constant.2.clone.perm_hbm), custom_call_target="tpu_custom_call" | custom-call | tf_op jit(solution)/shard_map/em_pass/pallas_call | solution.py:634
  59.1 1.5 %copy.8 = f32[12,1152]{1,0:T(8,128)} copy(f32[12,1152]{1,0:T(8,128)} %get-tuple-element.4) | data formatting | bytes 110592
  60.6 1.1 %copy.9 = f32[12]{0:T(128)} copy(f32[12]{0:T(128)} %get-tuple-element.5) | data formatting | bytes 96

commit v4 on v3

--- a/solution.py
+++ b/solution.py
@@ -1,5 +1,4 @@
 import math
-import numpy as np
 import jax
 import jax.numpy as jnp
 from jax import lax
@@ -162,8 +161,8 @@
 
 
 def kernel(
-    prior, images_hbm, refs, perm_hbm, out, out_mass,
-    images, perm, rows16, tload, x5, xh, tbuf, tf, tmix, offs, sh, stat, lh, mass, cf, cmix,
+    prior_hbm, images_hbm, refs, out, out_mass,
+    prior, images, perm, rows16, tload, x5, xh, tbuf, tf, tmix, offs, sh, stat, lh, mass, cf, cmix,
     own_a, own_b, own_c, s1a, s1b, s1c, r1a, r1b, r1c, s2a, s2b, s2c, r2a, r2b, r2c, s3a, s3b, s3c, r3a, r3b, r3c,
     load_sem, send_sem, recv_sem, off_send, off_recv, pair_send, pair_recv, rs_send, rs_recv,
 ):
@@ -186,8 +185,8 @@
         c = pltpu.make_async_copy(refs.at[pl.ds(36 * k // 16 * 16, 16)], rows16.at[k], load_sem.at[k])
         c.start()
         loads.append(c)
-    load_perm = pltpu.make_async_copy(perm_hbm, perm, load_sem.at[12])
-    load_perm.start()
+    load_prior = pltpu.make_async_copy(prior_hbm, prior, load_sem.at[12])
+    load_prior.start()
     load_images = pltpu.make_async_copy(images_hbm, images, load_sem.at[13])
     load_images.start()
 
@@ -202,7 +201,20 @@
     partners = [along(a, r) for a in range(3) for r in range(1, 4)] + [away(d) for d in (3, 5, 7)] + [sibling]
     for p in partners:
         pl.semaphore_signal(barrier, inc=1, device_id=p, device_id_type=MESH)
-    pl.semaphore_wait(barrier, len(partners))
+    def permutation(n, c):
+        i = n * 128 + lax.broadcasted_iota(jnp.int32, (128, 128), 0)
+        cycle = jnp.zeros_like(i)
+        for q in range(1, 8):
+            cycle = cycle + jnp.where(i >= ANG * q, 1, 0)
+        i = i - ANG * cycle
+        to = (i >> 2) * 32 + cycle * 4 + (i & 3) - lane((128, 128))
+        for v in range(9):
+            perm[pl.ds(pl.multiple_of(n * 128, 128), 128), v * 128 : v * 128 + 128] = jnp.where(
+                to == 128 * v, 1.0, 0.0
+            ).astype(BF16)
+        return c
+
+    lax.fori_loop(0, 9, permutation, 0)
 
     for c in loads:
         c.wait()
@@ -220,6 +232,7 @@
         tload[g * 16 : (g + 1) * 16, :] = t.astype(BF16)
     half_norm = 0.5 * jnp.sum(norm, axis=1, keepdims=True)
     rowid = lax.broadcasted_iota(jnp.int32, (16, 128), 0)
+    load_prior.wait()
     pri = jnp.ones((16, 128), F32)
     for k in range(12):
         pri = jnp.where(rowid == k, prior[k], pri)
@@ -227,8 +240,6 @@
     offs[slot] = jnp.log(pri) - half_norm
 
     sub8 = lax.broadcasted_iota(jnp.int32, (8, 128), 0)
-
-    load_perm.wait()
 
     def arrange(v, c):
         o = dot(tload[...], perm[:, pl.ds(pl.multiple_of(v * 128, 128), 128)])
@@ -242,27 +253,33 @@
 
     lax.fori_loop(0, 9, arrange, 0, unroll=9)
 
-    def piece(s, half):
-        return tbuf.at[s, pl.ds(432 * half, 432)]
+    pl.semaphore_wait(barrier, len(partners))
+
+    PIECES = ((0, 224), (224, 208), (432, 224), (656, 208))
+
+    def piece(s, p):
+        return tbuf.at[s, pl.ds(*PIECES[p])]
 
     started = []
 
-    def send(s, half, target, n):
+    def send(s, p, target, n):
         c = pltpu.make_async_remote_copy(
-            piece(s, half), piece(s, half), send_sem.at[n], recv_sem.at[n], device_id=target, device_id_type=MESH
+            piece(s, p), piece(s, p), send_sem.at[n], recv_sem.at[n], device_id=target, device_id_type=MESH
         )
         c.start()
         started.append(c)
 
-    def arrived(s, half, n):
-        pltpu.make_async_copy(piece(s, half), piece(s, half), recv_sem.at[n]).wait()
-
-    send(slot, 0, to_xp, 0)
-    send(slot, 1, to_xm, 2)
-    send(slot, 0, to_yp, 6)
-    send(slot, 1, to_ym, 7)
-    send(slot, 1, to_xp, 1)
-    send(slot, 0, to_xm, 3)
+    def arrived(s, p, n):
+        pltpu.make_async_copy(piece(s, p), piece(s, p), recv_sem.at[n]).wait()
+
+    for k in range(2):
+        send(slot, k, to_xp, k)
+        send(slot, 2 + k, to_xm, 6 + k)
+        send(slot, k, to_yp, 12 + k)
+        send(slot, 2 + k, to_ym, 14 + k)
+    for k in range(2):
+        send(slot, 2 + k, to_xp, 2 + k)
+        send(slot, k, to_xm, 4 + k)
     off_copies = []
     for d in range(1, 8):
         c = pltpu.make_async_remote_copy(
@@ -290,12 +307,13 @@
     )
     swap.start()
 
-    arrived(s_m, 0, 0)
-    send(s_m, 0, to_xp, 4)
-    send(s_m, 0, to_yp, 8)
-    arrived(s_p, 1, 2)
-    send(s_p, 1, to_xm, 5)
-    send(s_p, 1, to_ym, 9)
+    for k in range(2):
+        arrived(s_m, k, k)
+        send(s_m, k, to_xp, 8 + k)
+        send(s_m, k, to_yp, 16 + k)
+        arrived(s_p, 2 + k, 6 + k)
+        send(s_p, 2 + k, to_xm, 10 + k)
+        send(s_p, 2 + k, to_ym, 22 + k)
 
     def image_spectra(c):
         def step(n, carry):
@@ -314,75 +332,84 @@
         lax.fori_loop(0, 8, step, 0)
 
     image_spectra(core)
-    arrived(s_p, 0, 3)
-    send(s_p, 0, to_yp, 10)
-    arrived(s_m, 1, 1)
-    send(s_m, 1, to_ym, 11)
+    for k in range(2):
+        arrived(s_p, k, 4 + k)
+        send(s_p, k, to_yp, 20 + k)
+        arrived(s_m, 2 + k, 2 + k)
+        send(s_m, 2 + k, to_ym, 18 + k)
     swap.wait()
     image_spectra(1 - core)
-    arrived(s_2, 0, 4)
-    send(s_2, 0, to_yp, 12)
-    arrived(s_2, 1, 5)
-    send(s_2, 1, to_ym, 13)
-
-    def template_spectra(xx, ll):
-        s = xx * 2 + ll
+    for k in range(2):
+        arrived(s_2, k, 8 + k)
+        send(s_2, k, to_yp, 24 + k)
+        arrived(s_2, 2 + k, 10 + k)
+        send(s_2, 2 + k, to_ym, 26 + k)
+
+    def distance(i):
+        return jnp.where(i == 3, 2, jnp.where(i == 2, 3, i))
+
+    def row(i, part):
+        return jnp.where(i == 3, 72 + 8 * part, 24 * part + 8 * i)
+
+    def template_spectra(i, ll):
+        s = (x + distance(i)) % 4 * 2 + ll
         raw = []
         for b in range(HALF):
             two = tbuf[s, 48 * b : 48 * b + 48, :].astype(F32)
             raw += [two[:24], two[24:]]
         p = forward36(raw)
-        at = pl.ds(pl.multiple_of(ll * 32 + xx * 8, 8), 8)
+        at = pl.ds(pl.multiple_of(row(i, ll), 8), 8)
         for f in range(HALF):
             for ri in range(2):
                 v = p[f][ri]
                 tf[f, ri, at, 0:128] = v[0:8]
                 tf[f, ri, at, 128:256] = v[8:16]
-                tmix[s, f, ri] = v[16:24]
-
-    def own_row(n, c):
-        template_spectra((x + n) % 4, yl)
+                tmix[i, ll, f, ri] = v[16:24]
+
+    def score_part(members, lo, hi):
+        count = hi - lo
+
+        def score(f, c):
+            for ri in range(2):
+                for i in members:
+                    a, b = tmix[i, 0, f, ri], tmix[i, 1, f, ri]
+                    at = 88 if i == 3 else 48 + 8 * i
+                    tf[f, ri, at : at + 8, 0:128] = jnp.where(sub8 < 4, a, pltpu.roll(b, 4, 0))
+                    tf[f, ri, at : at + 8, 128:256] = jnp.where(sub8 < 4, pltpu.roll(a, 4, 0), b)
+            high, low = split(jnp.concatenate([tf[f, 0, lo:hi, :], tf[f, 1, lo:hi, :]], axis=0))
+            m = dot(high, xh[f, 0], NT) + (dot(low, xh[f, 0], NT) + dot(high, xh[f, 1], NT))
+            rr, ri_, ir, ii = m[:count, :128], m[:count, 128:], m[count:, :128], m[count:, 128:]
+            first = f == 0
+            sh[2 * f, lo:hi, :] = jnp.where(first, rr, rr + ii)
+            sh[2 * f + 1, lo:hi, :] = jnp.where(first, ii, ri_ - ir)
+            return c
+
+        lax.fori_loop(0, HALF, score, 0, unroll=6)
+
+    def own_row(i, c):
+        template_spectra(i, yl)
+        return c
+
+    def other_row(i, c):
+        template_spectra(i, 1 - yl)
         return c
 
     lax.fori_loop(0, 4, own_row, 0)
-    arrived(o_0, 0, 6)
-    arrived(o_0, 1, 7)
-    arrived(o_m, 0, 8)
-    arrived(o_p, 1, 9)
-    arrived(o_p, 0, 10)
-    arrived(o_m, 1, 11)
-    arrived(o_2, 0, 12)
-    arrived(o_2, 1, 13)
-
-    def other_row(n, c):
-        template_spectra((x + n) % 4, 1 - yl)
-        return c
-
-    lax.fori_loop(0, 4, other_row, 0)
+    for p in range(4):
+        arrived(o_0, p, 12 + p)
+    for p in range(4):
+        arrived(o_m, p, 16 + p)
+        arrived(o_p, p, 20 + p)
+    lax.fori_loop(0, 3, other_row, 0)
+    score_part((0, 1, 2), 0, 72)
+    for p in range(4):
+        arrived(o_2, p, 24 + p)
+    lax.fori_loop(3, 4, other_row, 0)
+    score_part((3,), 72, 96)
     for c in off_copies:
         c.wait()
 
-    def score(f, c):
-        for ri in range(2):
-            mix = [tmix[s, f, ri] for s in range(8)]
-            for xx in range(4):
-                a, b = mix[2 * xx], mix[2 * xx + 1]
-                tf[f, ri, 64 + 8 * xx : 72 + 8 * xx, 0:128] = jnp.where(sub8 < 4, a, pltpu.roll(b, 4, 0))
-                tf[f, ri, 64 + 8 * xx : 72 + 8 * xx, 128:256] = jnp.where(sub8 < 4, pltpu.roll(a, 4, 0), b)
-        rh, rl = split(tf[f, 0])
-        ih, il = split(tf[f, 1])
-        high = jnp.concatenate([rh, ih], axis=0)
-        low = jnp.concatenate([rl, il], axis=0)
-        m = dot(high, xh[f, 0], NT) + (dot(low, xh[f, 0], NT) + dot(high, xh[f, 1], NT))
-        rr, ri_, ir, ii = m[:96, :128], m[:96, 128:], m[96:, :128], m[96:, 128:]
-        first = f == 0
-        sh[2 * f] = jnp.where(first, rr, rr + ii)
-        sh[2 * f + 1] = jnp.where(first, ii, ri_ - ir)
-        return c
-
-    lax.fori_loop(0, HALF, score, 0, unroll=6)
-
-    def to_turns(xx, off, rows, top):
+    def to_turns(off, rows, top):
         p = [(sh[2 * f, rows, :], sh[2 * f + 1, rows, :]) for f in range(HALF)]
         s = inverse36(p)
         for r in range(36):
@@ -392,12 +419,13 @@
         return top
 
     def rows_of(n, c):
-        lo, hi = n % 4, n // 4
-        plain = offs[lo * 2 + jnp.minimum(hi, 1)]
-        a, b = offs[lo * 2], offs[lo * 2 + 1]
+        i = jnp.where(n < 9, n % 3, 3)
+        part = jnp.where(n < 9, n // 3, n - 9)
+        at = (x + distance(i)) % 4 * 2
+        a, b = offs[at], offs[at + 1]
         last = jnp.where(sub8 < 4, a[8:], pltpu.roll(b[8:], 4, 0))
-        off = jnp.where(hi == 2, last, plain[:8])
-        return to_turns(lo, off, pl.ds(pl.multiple_of(n * 8, 8), 8), c)
+        off = jnp.where(part == 0, a[:8], jnp.where(part == 1, b[:8], last))
+        return to_turns(off, pl.ds(pl.multiple_of(n * 8, 8), 8), c)
 
     top8 = lax.fori_loop(0, 12, rows_of, jnp.full((8, 128), -jnp.inf, F32))
     top = jnp.max(top8, axis=0, keepdims=True)
@@ -451,27 +479,36 @@
         for h in range(2):
             t = turn32([v[:, h * 128 : h * 128 + 128] for v in comps])
             for zz in range(4):
-                for xx in range(4):
-                    cf[zz, h, xx, 0, at, :] = t[zz][8 * xx : 8 * xx + 8]
-                    cf[zz, h, xx, 1, at, :] = t[zz][32 + 8 * xx : 40 + 8 * xx]
-                    cmix[zz, h, xx, u] = t[zz][64 + 8 * xx : 72 + 8 * xx]
+                for i in range(4):
+                    xx = (x + (0, 1, 3, 2)[i]) % 4
+                    r = [72 + 8 * p if i == 3 else 24 * p + 8 * i for p in range(3)]
+                    cf[zz, h, xx, 0, at, :] = t[zz][r[0] : r[0] + 8]
+                    cf[zz, h, xx, 1, at, :] = t[zz][r[1] : r[1] + 8]
+                    cmix[zz, h, xx, u] = t[zz][r[2] : r[2] + 8]
         return c
 
     place = (x, y, z)
     copies = []
 
-    def stage(n, axis, src, dst):
-        group = []
-        for r in range(1, 4):
-            c = pltpu.make_async_remote_copy(
-                src.at[(place[axis] + r) % 4], dst.at[r],
-                rs_send.at[3 * n + r - 1], rs_recv.at[3 * n + r - 1],
-                device_id=along(axis, r), device_id_type=MESH,
-            )
-            c.start()
-            group.append(c)
-            copies.append(c)
-        return group
+    ORDER = (2, 1, 3, 0)
+
+    def go(n, axis, r, src, dst):
+        c = pltpu.make_async_remote_copy(
+            src, dst, rs_send.at[n], rs_recv.at[n], device_id=along(axis, r), device_id_type=MESH
+        )
+        c.start()
+        copies.append(c)
+        return c
+
+    def first_stage(share, axis, second, src, dst):
+        groups = {}
+        for k in ORDER:
+            to = (place[second] + k) % 4
+            groups[k] = [
+                go(12 * share + 3 * k + r - 1, axis, r, src.at[(place[axis] + r) % 4, to], dst.at[r, to])
+                for r in range(1, 4)
+            ]
+        return groups
 
     def landed(group):
         for c in group:
@@ -495,9 +532,9 @@
             a, b = mixes[u], mixes[u + 1]
             tails[0].append(jnp.where(sub8 < 4, a, pltpu.roll(b, 4, 0)))
             tails[1].append(jnp.where(sub8 < 4, pltpu.roll(a, 4, 0), b))
-        mm = mass[pl.ds(pl.multiple_of(64 + 8 * xx, 8), 8), :]
-        m0 = mass[pl.ds(pl.multiple_of(8 * xx, 8), 8), :]
-        m1 = mass[pl.ds(pl.multiple_of(32 + 8 * xx, 8), 8), :]
+        d = (xx - x + 4) % 4
+        i = distance(d)
+        m0, m1, mm = (mass[pl.ds(pl.multiple_of(row(i, p), 8), 8), :] for p in range(3))
         for ll, (m8, m4, last) in enumerate(
             ((m0, pltpu.roll(mm, 4, 0), mixes[8]), (m1, mm, pltpu.roll(mixes[8], 4, 0)))
         ):
@@ -522,11 +559,11 @@
 
     lax.fori_loop(0, 6, sums, 0, unroll=3)
     lax.fori_loop(0, 32, pack_a, 0)
-    g1a = stage(0, 0, s1a, r1a)
+    g1a = first_stage(0, 0, 1, s1a, r1a)
     lax.fori_loop(6, 9, sums, 0, unroll=3)
     lax.fori_loop(0, 32, pack_bc, 0)
-    g1b = stage(1, 1, s1b, r1b)
-    g1c = stage(2, 2, s1c, r1c)
+    g1b = first_stage(1, 1, 2, s1b, r1b)
+    g1c = first_stage(2, 2, 0, s1c, r1c)
 
     def keep_a(n, c):
         for ll in range(2):
@@ -547,39 +584,36 @@
     lax.fori_loop(0, 16, keep_b, 0)
     lax.fori_loop(0, 8, keep_c, 0)
 
-    def add_first(own, got, to):
-        def step(n, c):
-            i, j = n // 4, n % 4
-            to[i, j] = own[i, j] + (got[1, i, j].astype(F32) + got[2, i, j].astype(F32)) + got[3, i, j].astype(F32)
-            return c
-
-        lax.fori_loop(0, 16, step, 0)
-
-    def add_second(held, got, to, axis):
+    shares = (
+        (g1a, own_a, r1a, s2a, r2a, s3a, r3a, 1, 2),
+        (g1b, own_b, r1b, s2b, r2b, s3b, r3b, 2, 0),
+        (g1c, own_c, r1c, s2c, r2c, s3c, r3c, 0, 1),
+    )
+    g2 = ([], [], [])
+    for k in ORDER:
+        for share, (g1, own, r1, s2, r2, s3, r3, second, third) in enumerate(shares):
+            landed(g1[k])
+            to = (place[second] + k) % 4
+            for j in range(4):
+                s2[to, j] = own[to, j] + (r1[1, to, j].astype(F32) + r1[2, to, j].astype(F32)) + r1[3, to, j].astype(F32)
+            if k:
+                g2[share].append(go(36 + 3 * share + k - 1, second, k, s2.at[to], r2.at[k]))
+    g3 = []
+    for share, (g1, own, r1, s2, r2, s3, r3, second, third) in enumerate(shares):
+        landed(g2[share])
         for j in range(4):
-            to[j] = held[place[axis], j] + (got[1, j] + got[2, j]) + got[3, j]
+            s3[j] = s2[place[second], j] + (r2[1, j] + r2[2, j]) + r2[3, j]
+        g3.append(
+            [
+                go(45 + 3 * share + k - 1, third, k, s3.at[(place[third] + k) % 4], r3.at[k])
+                for k in range(1, 4)
+            ]
+        )
 
     def add_third(held, got, axis):
         return held[place[axis]] + (got[1] + got[2]) + got[3]
 
-    landed(g1a)
-    add_first(own_a, r1a, s2a)
-    g2a = stage(3, 1, s2a, r2a)
-    landed(g1b)
-    add_first(own_b, r1b, s2b)
-    g2b = stage(4, 2, s2b, r2b)
-    landed(g1c)
-    add_first(own_c, r1c, s2c)
-    g2c = stage(5, 0, s2c, r2c)
-    landed(g2a)
-    add_second(s2a, r2a, s3a, 1)
-    g3a = stage(6, 2, s3a, r3a)
-    landed(g2b)
-    add_second(s2b, r2b, s3b, 2)
-    g3b = stage(7, 0, s3b, r3b)
-    landed(g2c)
-    add_second(s2c, r2c, s3c, 0)
-    g3c = stage(8, 1, s3c, r3c)
+    g3a, g3b, g3c = g3
     landed(g3a)
     part_a = add_third(s3a, r3a, 2)
     landed(g3b)
@@ -618,25 +652,17 @@
         c.wait_send()
 
 
-def column_order():
-    q, b, c = np.meshgrid(np.arange(8), np.arange(ROT), np.arange(TURN), indexing="ij")
-    perm = np.zeros((BAND, BAND), np.float32)
-    perm[(q * ANG + b * TURN + c).ravel(), (b * 32 + q * 4 + c).ravel()] = 1
-    return perm
-
-
 def per_device(images, references, class_prior):
-    perm = jnp.asarray(column_order(), BF16)
-    vmem = pl.BlockSpec(memory_space=pltpu.VMEM)
     hbm = pl.BlockSpec(memory_space=pl.ANY)
     smem = pl.BlockSpec(memory_space=pltpu.SMEM)
     rows = (48, 32, 32)
     return pl.pallas_call(
         kernel,
         out_shape=(jax.ShapeDtypeStruct((12, BAND), F32), jax.ShapeDtypeStruct((12,), F32)),
-        in_specs=[smem, hbm, hbm, hbm],
+        in_specs=[hbm, hbm, hbm],
         out_specs=(pl.BlockSpec(memory_space=pltpu.VMEM), smem),
         scratch_shapes=[
+            pltpu.SMEM((12,), F32),
             pltpu.VMEM((64, 9216), BF16),
             pltpu.VMEM((BAND, BAND), BF16),
             pltpu.VMEM((12, 16, 9216), BF16),
@@ -645,7 +671,7 @@
             pltpu.VMEM((HALF, 2, 256, 256), BF16),
             pltpu.VMEM((8, 864, 128), BF16),
             pltpu.VMEM((HALF, 2, 96, 256), F32),
-            pltpu.VMEM((8, HALF, 2, 8, 128), F32),
+            pltpu.VMEM((4, 2, HALF, 2, 8, 128), F32),
             pltpu.VMEM((8, 16, 128), F32),
             pltpu.VMEM((36, 96, 128), F32),
             pltpu.VMEM((2, 2, 8, 128), F32),
@@ -661,20 +687,20 @@
             *[pltpu.VMEM((4, r, 128), F32) for r in rows],
             *[pltpu.VMEM((4, r, 128), F32) for r in rows],
             pltpu.SemaphoreType.DMA((14,)),
-            pltpu.SemaphoreType.DMA((14,)),
-            pltpu.SemaphoreType.DMA((14,)),
+            pltpu.SemaphoreType.DMA((28,)),
+            pltpu.SemaphoreType.DMA((28,)),
             pltpu.SemaphoreType.DMA((8,)),
             pltpu.SemaphoreType.DMA((8,)),
             pltpu.SemaphoreType.DMA((2,)),
             pltpu.SemaphoreType.DMA((2,)),
-            pltpu.SemaphoreType.DMA((27,)),
-            pltpu.SemaphoreType.DMA((27,)),
+            pltpu.SemaphoreType.DMA((54,)),
+            pltpu.SemaphoreType.DMA((54,)),
         ],
         compiler_params=pltpu.CompilerParams(
             collective_id=0, has_side_effects=True, vmem_limit_bytes=56 * 1024 * 1024
         ),
         name="em_pass",
-    )(class_prior, images, references, perm)
+    )(class_prior, images, references)
 
 
 def solution(mesh):

time: 61.9 us -> 57.6 us (0.931)
  Pallas kernels: 58.4 us -> 54.2 us
    pallas_call x1, Pallas kernels: 58.4 us -> 54.2 us  [per_device(): pl.pallas_call(kernel, out_shape=(jax.ShapeDtypeStruct((12, BAND), F32),...]
where the time goes in v4:
time: 57.6 us; the launch traced here: 57.4 us
  Pallas kernels  54.2 us (94%)
  local copies, waits for them, and re-layouts  2.63 us (5%)
  between operations  0.64 us (1%)
    pallas_call x1, Pallas kernels, per_device(): pl.pallas_call(kernel, out_shape=(jax.ShapeDtypeStruct((12, BAND), F32),...  54.2 us
    unnamed x2, local copies, waits for them, and re-layouts  2.63 us

profile of v4, /device:TPU:0, one launch (start us, length us, event | category | flops | bytes accessed | tf_op | source)
XLA Modules:
  0.0 57.4 jit_solution(9318247025628350705)
XLA Ops:
  0.6 54.2 %em_pass.1 = (f32[12,1152]{1,0:T(8,128)}, f32[12]{0:T(128)}) custom-call(f32[12]{0:T(128)} %prior_hbm.1, bf16[64,9216]{1,0:T(8,128)(2,1)} %images_hbm.1, bf16[432,9216]{1,0:T(8,128)(2,1)} %refs.1), custom_call_target="tpu_custom_call" | custom-call | tf_op jit(solution)/shard_map/em_pass/pallas_call | solution.py:659
  54.8 1.5 %copy.7 = f32[12,1152]{1,0:T(8,128)} copy(f32[12,1152]{1,0:T(8,128)} %get-tuple-element.4) | data formatting | bytes 110592
  56.3 1.1 %copy.8 = f32[12]{0:T(128)} copy(f32[12]{0:T(128)} %get-tuple-element.5) | data formatting | bytes 96

commit v5 on v4

--- a/solution.py
+++ b/solution.py
@@ -401,11 +401,10 @@
         arrived(o_m, p, 16 + p)
         arrived(o_p, p, 20 + p)
     lax.fori_loop(0, 3, other_row, 0)
-    score_part((0, 1, 2), 0, 72)
     for p in range(4):
         arrived(o_2, p, 24 + p)
     lax.fori_loop(3, 4, other_row, 0)
-    score_part((3,), 72, 96)
+    score_part((0, 1, 2, 3), 0, 96)
     for c in off_copies:
         c.wait()
 
@@ -595,14 +594,18 @@
             landed(g1[k])
             to = (place[second] + k) % 4
             for j in range(4):
-                s2[to, j] = own[to, j] + (r1[1, to, j].astype(F32) + r1[2, to, j].astype(F32)) + r1[3, to, j].astype(F32)
+                total = own[to, j] + (r1[1, to, j].astype(F32) + r1[2, to, j].astype(F32)) + r1[3, to, j].astype(F32)
+                if k:
+                    s2[to, j] = total.astype(BF16)
+                else:
+                    own[to, j] = total
             if k:
                 g2[share].append(go(36 + 3 * share + k - 1, second, k, s2.at[to], r2.at[k]))
     g3 = []
     for share, (g1, own, r1, s2, r2, s3, r3, second, third) in enumerate(shares):
         landed(g2[share])
         for j in range(4):
-            s3[j] = s2[place[second], j] + (r2[1, j] + r2[2, j]) + r2[3, j]
+            s3[j] = own[place[second], j] + (r2[1, j].astype(F32) + r2[2, j].astype(F32)) + r2[3, j].astype(F32)
         g3.append(
             [
                 go(45 + 3 * share + k - 1, third, k, s3.at[(place[third] + k) % 4], r3.at[k])
@@ -682,8 +685,8 @@
             *[pltpu.VMEM((4, 4, r, 128), F32) for r in rows],
             *[pltpu.VMEM((4, 4, 4, r, 128), BF16) for r in rows],
             *[pltpu.VMEM((4, 4, 4, r, 128), BF16) for r in rows],
-            *[pltpu.VMEM((4, 4, r, 128), F32) for r in rows],
-            *[pltpu.VMEM((4, 4, r, 128), F32) for r in rows],
+            *[pltpu.VMEM((4, 4, r, 128), BF16) for r in rows],
+            *[pltpu.VMEM((4, 4, r, 128), BF16) for r in rows],
             *[pltpu.VMEM((4, r, 128), F32) for r in rows],
             *[pltpu.VMEM((4, r, 128), F32) for r in rows],
             pltpu.SemaphoreType.DMA((14,)),

time: 57.6 us -> 54.4 us (0.944)
  Pallas kernels: 54.2 us -> 51 us
    pallas_call x1, Pallas kernels: 54.2 us -> 51 us  [per_device(): pl.pallas_call(kernel, out_shape=(jax.ShapeDtypeStruct((12, BAND), F32),...]
where the time goes in v5:
time: 54.4 us; the launch traced here: 54.3 us
  Pallas kernels  51 us (94%)
  local copies, waits for them, and re-layouts  2.63 us (5%)
  between operations  0.64 us (1%)
    pallas_call x1, Pallas kernels, per_device(): pl.pallas_call(kernel, out_shape=(jax.ShapeDtypeStruct((12, BAND), F32),...  51 us
    unnamed x2, local copies, waits for them, and re-layouts  2.63 us

profile of v5, /device:TPU:0, one launch (start us, length us, event | category | flops | bytes accessed | tf_op | source)
XLA Modules:
  0.0 54.3 jit_solution(14596456951795025528)
XLA Ops:
  0.6 51.0 %em_pass.1 = (f32[12,1152]{1,0:T(8,128)}, f32[12]{0:T(128)}) custom-call(f32[12]{0:T(128)} %prior_hbm.1, bf16[64,9216]{1,0:T(8,128)(2,1)} %images_hbm.1, bf16[432,9216]{1,0:T(8,128)(2,1)} %refs.1), custom_call_target="tpu_custom_call" | custom-call | tf_op jit(solution)/shard_map/em_pass/pallas_call | solution.py:662
  51.6 1.5 %copy.7 = f32[12,1152]{1,0:T(8,128)} copy(f32[12,1152]{1,0:T(8,128)} %get-tuple-element.4) | data formatting | bytes 110592
  53.2 1.1 %copy.8 = f32[12]{0:T(128)} copy(f32[12]{0:T(128)} %get-tuple-element.5) | data formatting | bytes 96

commit v6 on v5

--- a/solution.py
+++ b/solution.py
@@ -377,7 +377,8 @@
                     tf[f, ri, at : at + 8, 0:128] = jnp.where(sub8 < 4, a, pltpu.roll(b, 4, 0))
                     tf[f, ri, at : at + 8, 128:256] = jnp.where(sub8 < 4, pltpu.roll(a, 4, 0), b)
             high, low = split(jnp.concatenate([tf[f, 0, lo:hi, :], tf[f, 1, lo:hi, :]], axis=0))
-            m = dot(high, xh[f, 0], NT) + (dot(low, xh[f, 0], NT) + dot(high, xh[f, 1], NT))
+            m = dot(jnp.concatenate([high, low], axis=0), xh[f, 0], NT)
+            m = m[: 2 * count] + (m[2 * count :] + dot(high, xh[f, 1], NT))
             rr, ri_, ir, ii = m[:count, :128], m[:count, 128:], m[count:, :128], m[count:, 128:]
             first = f == 0
             sh[2 * f, lo:hi, :] = jnp.where(first, rr, rr + ii)
@@ -472,7 +473,7 @@
         for ff in range(2):
             f = 2 * u + ff
             a, b = lh[f, 0], lh[f, 1]
-            m = dot(a, xh[f, 0]) + (dot(b, xh[f, 0]) + dot(a, xh[f, 1]))
+            m = dot(jnp.concatenate([a, b, a], axis=1), jnp.concatenate([xh[f, 0], xh[f, 0], xh[f, 1]], axis=0))
             comps += [m[:96], m[96:]]
         at = pl.ds(pl.multiple_of(8 * u, 8), 8)
         for h in range(2):
@@ -556,7 +557,7 @@
             s1c[zz, xx, 2 * hh + ll] = c_.astype(BF16)
         return c
 
-    lax.fori_loop(0, 6, sums, 0, unroll=3)
+    lax.fori_loop(0, 6, sums, 0, unroll=6)
     lax.fori_loop(0, 32, pack_a, 0)
     g1a = first_stage(0, 0, 1, s1a, r1a)
     lax.fori_loop(6, 9, sums, 0, unroll=3)

time: 54.4 us -> 53.6 us (0.985)
  Pallas kernels: 51 us -> 50.2 us
    pallas_call x1, Pallas kernels: 51 us -> 50.2 us  [per_device(): pl.pallas_call(kernel, out_shape=(jax.ShapeDtypeStruct((12, BAND), F32),...]
where the time goes in v6:
time: 53.6 us; the launch traced here: 53.4 us
  Pallas kernels  50.2 us (94%)
  local copies, waits for them, and re-layouts  2.63 us (5%)
  between operations  0.64 us (1%)
    pallas_call x1, Pallas kernels, per_device(): pl.pallas_call(kernel, out_shape=(jax.ShapeDtypeStruct((12, BAND), F32),...  50.2 us
    unnamed x2, local copies, waits for them, and re-layouts  2.63 us

profile of v6, /device:TPU:0, one launch (start us, length us, event | category | flops | bytes accessed | tf_op | source)
XLA Modules:
  0.0 53.4 jit_solution(7170636171653154534)
XLA Ops:
  0.6 50.2 %em_pass.1 = (f32[12,1152]{1,0:T(8,128)}, f32[12]{0:T(128)}) custom-call(f32[12]{0:T(128)} %prior_hbm.1, bf16[64,9216]{1,0:T(8,128)(2,1)} %images_hbm.1, bf16[432,9216]{1,0:T(8,128)(2,1)} %refs.1), custom_call_target="tpu_custom_call" | custom-call | tf_op jit(solution)/shard_map/em_pass/pallas_call | solution.py:663
  50.8 1.5 %copy.7 = f32[12,1152]{1,0:T(8,128)} copy(f32[12,1152]{1,0:T(8,128)} %get-tuple-element.4) | data formatting | bytes 110592
  52.3 1.1 %copy.8 = f32[12]{0:T(128)} copy(f32[12]{0:T(128)} %get-tuple-element.5) | data formatting | bytes 96

commit v7 on v6

--- a/solution.py
+++ b/solution.py
@@ -385,7 +385,7 @@
             sh[2 * f + 1, lo:hi, :] = jnp.where(first, ii, ri_ - ir)
             return c
 
-        lax.fori_loop(0, HALF, score, 0, unroll=6)
+        lax.fori_loop(0, HALF, score, 0, unroll=9)
 
     def own_row(i, c):
         template_spectra(i, yl)
@@ -438,7 +438,7 @@
             c = c + e
         return c
 
-    total = jnp.sum(lax.fori_loop(0, 12, raise_, jnp.zeros((8, 128), F32)), axis=0, keepdims=True)
+    total = jnp.sum(lax.fori_loop(0, 12, raise_, jnp.zeros((8, 128), F32), unroll=2), axis=0, keepdims=True)
     stat[0, 0] = jnp.broadcast_to(top, (8, 128))
     stat[0, 1] = jnp.broadcast_to(total, (8, 128))
     share = pltpu.make_async_remote_copy(
@@ -558,10 +558,10 @@
         return c
 
     lax.fori_loop(0, 6, sums, 0, unroll=6)
-    lax.fori_loop(0, 32, pack_a, 0)
+    lax.fori_loop(0, 32, pack_a, 0, unroll=4)
     g1a = first_stage(0, 0, 1, s1a, r1a)
     lax.fori_loop(6, 9, sums, 0, unroll=3)
-    lax.fori_loop(0, 32, pack_bc, 0)
+    lax.fori_loop(0, 32, pack_bc, 0, unroll=4)
     g1b = first_stage(1, 1, 2, s1b, r1b)
     g1c = first_stage(2, 2, 0, s1c, r1c)
 

time: 53.6 us -> 53 us (0.989)
  Pallas kernels: 50.2 us -> 49.6 us
    pallas_call x1, Pallas kernels: 50.2 us -> 49.6 us  [per_device(): pl.pallas_call(kernel, out_shape=(jax.ShapeDtypeStruct((12, BAND), F32),...]
where the time goes in v7:
time: 53 us; the launch traced here: 52.8 us
  Pallas kernels  49.6 us (94%)
  local copies, waits for them, and re-layouts  2.63 us (5%)
  between operations  0.64 us (1%)
    pallas_call x1, Pallas kernels, per_device(): pl.pallas_call(kernel, out_shape=(jax.ShapeDtypeStruct((12, BAND), F32),...  49.6 us
    unnamed x2, local copies, waits for them, and re-layouts  2.63 us

profile of v7, /device:TPU:0, one launch (start us, length us, event | category | flops | bytes accessed | tf_op | source)
XLA Modules:
  0.0 52.8 jit_solution(16936303454439912819)
XLA Ops:
  0.6 49.6 %em_pass.1 = (f32[12,1152]{1,0:T(8,128)}, f32[12]{0:T(128)}) custom-call(f32[12]{0:T(128)} %prior_hbm.1, bf16[64,9216]{1,0:T(8,128)(2,1)} %images_hbm.1, bf16[432,9216]{1,0:T(8,128)(2,1)} %refs.1), custom_call_target="tpu_custom_call" | custom-call | tf_op jit(solution)/shard_map/em_pass/pallas_call | solution.py:663
  50.2 1.5 %copy.7 = f32[12,1152]{1,0:T(8,128)} copy(f32[12,1152]{1,0:T(8,128)} %get-tuple-element.4) | data formatting | bytes 110592
  51.7 1.1 %copy.8 = f32[12]{0:T(128)} copy(f32[12]{0:T(128)} %get-tuple-element.5) | data formatting | bytes 96
